TPU v7x, 256 devices: a whole 4x4x8 slice. The times are simulated.
256 devices in a mesh: grp: 16 (over x, y), exp: 16 (over z, core).
Axes of the slice: x: 4, y: 4, z: 8, core: 2. Of those that a mesh axis runs over, the one named last changes fastest.
Arguments:
- tokens: bfloat16 [32768, 2048], P(('grp', 'exp')), may hold values from -6 to 6
- cotangent: bfloat16 [32768, 2048], P(('grp', 'exp')), may hold values from -3 to 3
- timestep: int32 [32768], P(('grp', 'exp')), may hold values from 0 to 15
- shift_table: float32 [16, 2048], replicated, may hold values from -3 to 3
- scale_table: float32 [16, 2048], replicated, may hold values from -2.5 to 2.5
- gate_table: float32 [16, 2048], replicated, may hold values from -4 to 4
- chosen: int32 [16, 8, 256], P('grp'), may hold values from 0 to 2047, as said below
- combine: float32 [16, 8, 256], P('grp'), may hold values from 0.1 to 1
- w_gate: bfloat16 [16, 704, 2048], P('exp'), may hold values from -0.125 to 0.125
- w_up: bfloat16 [16, 704, 2048], P('exp'), may hold values from -0.125 to 0.125
- w_down: bfloat16 [16, 704, 2048], P('exp'), may hold values from -0.15625 to 0.15625
Outputs:
- d_tokens: bfloat16 [32768, 2048], P(('grp', 'exp'))
- d_combine: float32 [16, 16, 128], P('grp', 'exp')
- d_w_gate: bfloat16 [16, 704, 2048], P('exp', None, 'grp')
- d_w_up: bfloat16 [16, 704, 2048], P('exp', None, 'grp')
- d_w_down: bfloat16 [16, 704, 2048], P('exp', None, 'grp')
Inputs may be any that keep to these rules, and one draw needn't show every extreme that they name: Each list chosen[g, e, :] names 256 different tokens of group g; at most 32 of them lie among the 128 tokens of one device, and in every list some device's tokens supply exactly 32.
All inputs are finite; a program needn't handle non-finite values.
Results may differ from a plain program's by a relative error of at most 0.014.
Values may be sent and summed in bfloat16 or wider, within the bound.
A program may use at most 128 MiB of HBM per device.

v0:
```python
import jax
import jax.numpy as jnp
from jax import lax
from jax.sharding import PartitionSpec as P

EPSILON = 1e-06
CONTRACT_FIRST = (((0,), (0,)), ((), ()))
CONTRACT_SECOND = (((1,), (1,)), ((), ()))


def from_partner(shard, axis, apart):
    return lax.ppermute(shard, axis, [(i, i ^ 1 << apart) for i in range(lax.axis_size(axis))])


def layer_stats(tokens):
    values = tokens.astype(jnp.float32)
    centred = values - jnp.mean(values, axis=1, keepdims=True)
    inverse = lax.rsqrt(jnp.mean(centred * centred, axis=1, keepdims=True) + EPSILON)
    return (centred * inverse, inverse)


def table_rows(timestep, table):
    matches = (timestep[:, None] == jnp.arange(table.shape[0], dtype=jnp.int32)[None, :]).astype(
        jnp.float32
    )
    return jnp.dot(matches, table, precision=lax.Precision.HIGHEST)


def owner_plan(chosen_rows, tok_dev, peer_count):
    owners = chosen_rows // tok_dev
    local_row = chosen_rows - owners * tok_dev
    matches = (owners[:, :, None] == jnp.arange(peer_count, dtype=jnp.int32)[None, None, :]).astype(
        jnp.int32
    )
    before = jnp.cumsum(matches, axis=1) - matches
    place_in = jnp.sum(before * matches, axis=2)
    return (owners, local_row, place_in)


def pick_rows(values, send_table, tok_dev):
    taken_rows = jnp.take(values, jnp.minimum(send_table, tok_dev - 1), axis=0)
    return jnp.where((send_table < tok_dev)[:, None], taken_rows, jnp.zeros_like(taken_rows))


def expert_rows(rows_in, rows_grad, row_weight, gate_half, up_half, down_half):
    pre_gate = lax.dot_general(
        gate_half, rows_in, CONTRACT_SECOND, preferred_element_type=jnp.float32
    )
    pre_up = lax.dot_general(up_half, rows_in, CONTRACT_SECOND, preferred_element_type=jnp.float32)
    sigmoid_gate = jax.nn.sigmoid(pre_gate)
    silu_gate = pre_gate * sigmoid_gate
    hidden = (silu_gate * pre_up).astype(jnp.bfloat16)
    out_part = lax.dot_general(
        hidden, down_half, CONTRACT_FIRST, preferred_element_type=jnp.float32
    )
    inner_dots = jnp.sum(rows_grad.astype(jnp.float32) * out_part, axis=1)
    d_out = (row_weight[:, None] * rows_grad.astype(jnp.float32)).astype(jnp.bfloat16)
    d_hidden = lax.dot_general(
        down_half, d_out, CONTRACT_SECOND, preferred_element_type=jnp.float32
    )
    grad_down = jnp.dot(hidden, d_out, preferred_element_type=jnp.float32)
    d_gate = (d_hidden * pre_up * sigmoid_gate * (1.0 + pre_gate * (1.0 - sigmoid_gate))).astype(
        jnp.bfloat16
    )
    d_up = (d_hidden * silu_gate).astype(jnp.bfloat16)
    grad_gate = jnp.dot(d_gate, rows_in, preferred_element_type=jnp.float32)
    grad_up = jnp.dot(d_up, rows_in, preferred_element_type=jnp.float32)
    d_rows = lax.dot_general(
        d_gate, gate_half, CONTRACT_FIRST, preferred_element_type=jnp.float32
    ) + lax.dot_general(d_up, up_half, CONTRACT_FIRST, preferred_element_type=jnp.float32)
    return (inner_dots, grad_gate, grad_up, grad_down, d_rows)


def on_device(
    tokens,
    cotangent,
    timestep,
    shift_table,
    scale_table,
    gate_table,
    chosen,
    combine,
    w_gate,
    w_up,
    w_down,
):
    device = lax.axis_index("exp")
    peer_count = lax.axis_size("exp")
    groups = lax.axis_size("grp")
    tok_dev = tokens.shape[0]
    features = tokens.shape[1]
    capacity = chosen.shape[2]
    slot_rows = 2 * capacity // peer_count
    buffer_rows = peer_count * slot_rows
    expert_count = peer_count // 2
    chosen_rows = chosen[0]
    weights_all = combine[0]
    normed, inverse = layer_stats(tokens)
    scale_rows = table_rows(timestep, scale_table)
    modulated = (normed * (1.0 + scale_rows) + table_rows(timestep, shift_table)).astype(
        jnp.bfloat16
    )
    scaled = (table_rows(timestep, gate_table) * cotangent.astype(jnp.float32)).astype(jnp.bfloat16)
    owners, local_row, place_in = owner_plan(chosen_rows, tok_dev, peer_count)
    expert_ids = jnp.arange(chosen_rows.shape[0], dtype=jnp.int32)[:, None]
    is_mine = owners == device
    full_table = jnp.full((buffer_rows,), tok_dev, jnp.int32)
    for half_index in range(2):
        targets = (2 * expert_ids + half_index) * slot_rows + place_in
        full_table = full_table.at[jnp.where(is_mine, targets, buffer_rows)].set(
            local_row, mode="drop"
        )
    expert_table = full_table.reshape(expert_count, 2, slot_rows)[:, 0].reshape(
        expert_count * slot_rows
    )
    half_bit = device % 2
    recv_in, recv_grad = (
        lax.all_to_all(
            pick_rows(modulated, full_table, tok_dev).reshape(peer_count, slot_rows, features),
            "exp",
            split_axis=0,
            concat_axis=0,
            tiled=True,
        ),
        lax.all_to_all(
            pick_rows(scaled, full_table, tok_dev).reshape(peer_count, slot_rows, features),
            "exp",
            split_axis=0,
            concat_axis=0,
            tiled=True,
        ),
    )
    expert_id = device // 2
    my_owner = lax.dynamic_index_in_dim(owners, expert_id, 0, keepdims=False)
    my_place = lax.dynamic_index_in_dim(place_in, expert_id, 0, keepdims=False)
    my_weight = lax.dynamic_index_in_dim(weights_all, expert_id, 0, keepdims=False)
    positions = my_owner * slot_rows + my_place
    flat_in = recv_in.reshape(buffer_rows, features)
    flat_grad = recv_grad.reshape(buffer_rows, features)
    inner_dots, grad_gate, grad_up, grad_down, d_rows = expert_rows(
        jnp.take(flat_in, positions, axis=0),
        jnp.take(flat_grad, positions, axis=0),
        my_weight,
        w_gate[0],
        w_up[0],
        w_down[0],
    )
    totals = inner_dots + from_partner(inner_dots, "exp", 0)
    d_back = jnp.zeros((buffer_rows, features), jnp.float32).at[positions].set(d_rows)
    d_blocks = d_back.reshape(peer_count, slot_rows, features)
    returned = lax.all_to_all(
        d_blocks.astype(jnp.bfloat16), "exp", split_axis=0, concat_axis=0, tiled=True
    ).astype(d_blocks.dtype)
    paired_sums = returned.reshape(expert_count, 2, slot_rows, features)
    expert_sums = (
        (paired_sums[:, 0] + paired_sums[:, 1])
        .astype(jnp.bfloat16)
        .reshape(expert_count * slot_rows, features)
    )
    d_modulated = (
        jnp.zeros((tok_dev, features), jnp.float32)
        .at[expert_table]
        .add(expert_sums.astype(jnp.float32), mode="drop")
    )
    d_normed = d_modulated * (1.0 + scale_rows)
    d_tokens = inverse * (
        d_normed
        - jnp.mean(d_normed, axis=1, keepdims=True)
        - normed * jnp.mean(d_normed * normed, axis=1, keepdims=True)
    )
    d_combine = lax.dynamic_slice_in_dim(totals, half_bit * (capacity // 2), capacity // 2)[
        None, None, :
    ]
    summed = (
        lax.psum_scatter(
            grad_gate.astype(jnp.bfloat16), "grp", scatter_dimension=1, tiled=True
        ).astype(jnp.float32),
        lax.psum_scatter(
            grad_up.astype(jnp.bfloat16), "grp", scatter_dimension=1, tiled=True
        ).astype(jnp.float32),
        lax.psum_scatter(
            grad_down.astype(jnp.bfloat16), "grp", scatter_dimension=1, tiled=True
        ).astype(jnp.float32),
    )
    d_w_gate = (summed[0] / groups).astype(jnp.bfloat16)[None]
    d_w_up = (summed[1] / groups).astype(jnp.bfloat16)[None]
    d_w_down = (summed[2] / groups).astype(jnp.bfloat16)[None]
    return (d_tokens.astype(jnp.bfloat16), d_combine, d_w_gate, d_w_up, d_w_down)


def solution(mesh):
    in_specs = (
        P(("grp", "exp"), None),
        P(("grp", "exp"), None),
        P(("grp", "exp")),
        P(),
        P(),
        P(),
        P("grp", None, None),
        P("grp", None, None),
        P("exp", None, None),
        P("exp", None, None),
        P("exp", None, None),
    )
    out_specs = (
        P(("grp", "exp"), None),
        P("grp", "exp", None),
        P("exp", None, "grp"),
        P("exp", None, "grp"),
        P("exp", None, "grp"),
    )
    return jax.shard_map(
        on_device, mesh=mesh, in_specs=in_specs, out_specs=out_specs, check_vma=False
    )
```

profile of v0, /device:TPU:1, one launch (start us, length us, event | category | flops | bytes accessed | tf_op | source)
XLA Modules:
  0.0 436.8 jit_solution(93082664674226808)
XLA Ops:
  7.2 0.9 add_select_fusion
  8.1 0.7 fusion.72
  8.8 4.6 %reduce-window.6 = s32[8,16,2,128]{3,1,2,0:T(8,128)S(1)} reduce-window(s32[8,16,2,128]{3,1,2,0:T(8,128)S(1)} %fusion.56, s32[]{:T(128)} %constant.106.clone.1), window={size=1x1x1x128 pad=0_0x0_0x0_0x127_0}, to_apply=%region_2.3 | reduce-window | flops 4161536 | bytes 262148 | tf_op jit(solution)/shard_map/reduce-window
  13.4 0.1 slice.28
  13.5 0.2 copy.22
  13.7 0.1 fusion.55
  13.9 0.8 fusion.65
  14.6 0.6 copy.34
  15.2 8.0 %scatter_custom_fusion = s32[512]{0:T(512)S(1)} fusion(s32[2048]{0:T(1024)S(1)} %bitcast.191, s32[2048]{0:T(1024)S(1)} %bitcast.188, s32[]{:T(128)} %constant.104.clone.1), kind=kCustom, calls=%fused_computation.133 | custom fusion | bytes 2052 | tf_op jit(solution)/shard_map/scatter | solution.py:110
  23.3 8.3 %scatter_fusion = s32[512]{0:T(512)S(1)} fusion(s32[512]{0:T(512)S(1)} %scatter_custom_fusion, s32[2048]{0:T(1024)} %bitcast.190, s32[2048]{0:T(1024)} %bitcast.189), kind=kCustom, calls=%fused_computation.5 | custom fusion | bytes 32768 | tf_op jit(solution)/shard_map/scatter | solution.py:110
  31.7 0.6 broadcast_compare_fusion
  32.3 0.2 convert_reduce_fusion
  32.5 0.3 fusion.47
  32.8 1.3 convolution_add_fusion.1
  34.1 0.6 fusion.18
  34.8 0.3 copy-done.4
  35.1 1.5 fusion.19
  36.6 6.3 %gather_fusion.2 = bf16[512,2048]{1,0:T(8,128)(2,1)} fusion(bf16[128,2048]{1,0:T(8,128)(2,1)} %fusion.19, s32[1024]{0:T(1024)S(1)} %pad_clamp_fusion.1), kind=kCustom, calls=%fused_computation.2.clone | custom fusion | bytes 4196352 | tf_op jit(solution)/shard_map/jit(_take)/gather | solution.py:41
  42.9 3.3 gather_fusion
  46.3 3.6 select_select_fusion.1
  49.8 60.9 %all_to_all.15 = bf16[16,32,2048]{2,1,0:T(8,128)(2,1)} all-to-all(bf16[16,32,2048]{2,1,0:T(8,128)(2,1)S(1)} %bitcast.183), channel_id=1, replica_groups=mesh['grp'=16,'exp'=16] {'exp'}, dimensions={0} | all-to-all | bytes 4194304 | tf_op jit(solution)/shard_map/all_to_all | solution.py:118
  110.7 4.3 all-to-all-start
  115.1 0.2 reduce-scatter.14.cloned.1.call-start
  115.5 0.7 constant_dynamic-slice_fusion
  116.2 0.7 compare_select_fusion.2
  116.9 5.3 %gather_fusion.3 = bf16[256,2048]{1,0:T(8,128)(2,1)} fusion(bf16[512,2048]{1,0:T(8,128)(2,1)} %bitcast.177, s32[1024]{0:T(1024)S(1)} %pad_clamp_fusion), kind=kCustom, calls=%fused_computation.3.clone | custom fusion | bytes 2098176 | tf_op jit(solution)/shard_map/jit(_take)/gather | solution.py:141
  122.2 40.5 %all-to-all-done = bf16[16,32,2048]{2,1,0:T(8,128)(2,1)} async-done(((bf16[16,32,2048]{2,1,0:T(8,128)(2,1)}), bf16[16,32,2048]{2,1,0:T(8,128)(2,1)}, u32[]{:S(2)}, u32[]{:S(2)}) %all-to-all-start) | async-done | bytes 2097184 | tf_op jit(solution)/shard_map/all_to_all | solution.py:125
  162.7 5.3 %gather_fusion.1 = bf16[256,2048]{1,0:T(8,128)(2,1)} fusion(bf16[512,2048]{1,0:T(8,128)(2,1)} %bitcast.12, s32[1024]{0:T(1024)S(1)} %pad_clamp_fusion), kind=kCustom, calls=%fused_computation.1.clone | custom fusion | bytes 2098176 | tf_op jit(solution)/shard_map/jit(_take)/gather | solution.py:142
  168.0 3.3 fusion.35
  171.3 1.1 fusion.29
  172.4 0.1 copy-done.5
  172.5 2.0 multiply_convert_fusion
  174.5 0.7 copy-done.8
  175.3 2.7 convolution_convert_fusion
  177.9 4.6 %copy.29 = bf16[704,2048]{0,1:T(8,128)(2,1)} copy(bf16[704,2048]{1,0:T(8,128)(2,1)} %convolution_convert_fusion) | data formatting | bytes 5767168
  182.6 0.3 reduce-scatter.12.cloned.1.call-start
  182.9 3.8 convolution_convert_fusion.1
  186.7 4.6 %copy.27 = bf16[704,2048]{0,1:T(8,128)(2,1)} copy(bf16[704,2048]{1,0:T(8,128)(2,1)} %convolution_convert_fusion.1) | data formatting | bytes 5767168
  191.3 2.9 fusion
  194.3 2.3 fusion.15
  196.6 5.1 %scatter_custom_fusion.2 = f32[512,2048]{1,0:T(8,128)} fusion(s32[256]{0:T(256)S(1)} %bitcast.197, f32[256,2048]{1,0:T(8,128)} %fusion.15, f32[]{:T(128)} %constant.67.clone.1), kind=kCustom, calls=%fused_computation.38 | custom fusion | bytes 4194816 | tf_op jit(solution)/shard_map/scatter | solution.py:149
  201.7 3.8 convert_element_type.96
  205.5 5.2 %all-to-all-start.2 = ((bf16[16,32,2048]{2,1,0:T(8,128)(2,1)}), bf16[16,32,2048]{2,1,0:T(8,128)(2,1)}, u32[]{:S(2)}, u32[]{:S(2)}) async-start(bf16[16,32,2048]{2,1,0:T(8,128)(2,1)} %bitcast.182), calls=%async_computation.2 | async-start | bytes 4194304 | tf_op jit(solution)/shard_map/all_to_all | solution.py:151
  210.8 3.8 convolution_convert_fusion.2
  214.5 4.7 %copy.25 = bf16[704,2048]{0,1:T(8,128)(2,1)} copy(bf16[704,2048]{1,0:T(8,128)(2,1)} %convolution_convert_fusion.2) | data formatting | bytes 5767168
  219.2 1.0 copy-done.9
  220.2 3.3 fusion.26
  223.5 0.2 collective-permute-start
  223.7 1.0 collective-permute-done
  224.7 0.6 dynamic-slice_bitcast_fusion
  225.3 34.5 %all-to-all-done.2 = bf16[16,32,2048]{2,1,0:T(8,128)(2,1)} async-done(((bf16[16,32,2048]{2,1,0:T(8,128)(2,1)}), bf16[16,32,2048]{2,1,0:T(8,128)(2,1)}, u32[]{:S(2)}, u32[]{:S(2)}) %all-to-all-start.2) | async-done | bytes 2097184 | tf_op jit(solution)/shard_map/all_to_all | solution.py:151
  259.8 2.1 convert.2
  261.9 1.3 fusion.21
  263.2 5.6 %scatter_custom_fusion.3 = f32[128,2048]{1,0:T(8,128)} fusion(s32[256]{0:T(256)S(1)} %bitcast.196, bf16[256,2048]{1,0:T(8,128)(2,1)} %bitcast.184, f32[]{:T(128)} %constant.67.clone.1), kind=kCustom, calls=%fused_computation.34 | custom fusion | flops 1048576 | bytes 2097156 | tf_op jit(solution)/shard_map/scatter-add | solution.py:163
  268.8 1.9 fusion.81
  270.8 1.2 fusion.46
  272.0 1.1 copy.30
  273.1 71.6 %reduce-scatter.12.cloned.1.call-done = bf16[128,704]{1,0:T(8,128)(2,1)} async-done(((bf16[2048,704]{1,0:T(8,128)(2,1)}), bf16[128,704]{1,0:T(8,128)(2,1)}) %reduce-scatter.12.cloned.1.call-update) | async-done | bytes 180240
  344.7 1.1 copy.28
  345.8 0.7 fusion.52
  346.5 0.7 fusion.51
  347.2 81.3 %reduce-scatter.10.cloned.1.call-done = bf16[128,704]{1,0:T(8,128)(2,1)} async-done(((bf16[2048,704]{1,0:T(8,128)(2,1)}), bf16[128,704]{1,0:T(8,128)(2,1)}) %reduce-scatter.10.cloned.1.call-update) | async-done | bytes 180240
  428.5 1.1 copy.26
  429.6 0.7 fusion.50
  (71 shorter events, 0.5 us)
Async XLA Ops:
  7.2 165.3 %copy-start = (bf16[1,704,2048]{2,1,0:T(8,128)(2,1)S(1)}, bf16[1,704,2048]{2,1,0:T(8,128)(2,1)}, u32[]{:S(2)}) copy-start(bf16[1,704,2048]{2,1,0:T(8,128)(2,1)} %param.24) | copy-start | bytes 8650756
  8.8 14.5 %copy-start.15 = (s32[1,2,8,128]{3,1,2,0:T(2,128)}, s32[1,2,8,128]{3,1,2,0:T(2,128)S(1)}, u32[]{:S(2)}) copy-start(s32[1,2,8,128]{3,1,2,0:T(2,128)S(1)} %copy.33) | copy-start | bytes 24580
  13.9 9.4 %copy-start.14 = (s32[8,256]{1,0:T(8,128)}, s32[8,256]{1,0:T(8,128)S(1)}, u32[]{:S(2)}) copy-start(s32[8,256]{1,0:T(8,128)S(1)} %fusion.55) | copy-start | bytes 24580
  23.3 9.0 %copy-start.1 = (bf16[128,2048]{1,0:T(8,128)(2,1)S(1)}, bf16[128,2048]{1,0:T(8,128)(2,1)}, u32[]{:S(2)}) copy-start(bf16[128,2048]{1,0:T(8,128)(2,1)} %param.15) | copy-start | bytes 1572868
  23.3 9.5 %copy-start.11 = (f32[16,2048]{1,0:T(8,128)S(1)}, f32[16,2048]{1,0:T(8,128)}, u32[]{:S(2)}) copy-start(f32[16,2048]{1,0:T(8,128)} %param.19) | copy-start | bytes 393220
  31.6 2.4 copy-start.10
  31.7 2.4 copy-start.12
  31.7 2.4 copy-start.18
  31.7 3.4 copy-start.2
  31.7 3.4 copy-start.13
  32.5 2.3 copy-start.16
  32.8 2.0 copy-start.19
  34.1 1.0 copy-start.4
  42.9 3.3 copy-start.21
  42.9 3.3 copy-start.22
  110.7 52.0 %all-to-all-start = ((bf16[16,32,2048]{2,1,0:T(8,128)(2,1)}), bf16[16,32,2048]{2,1,0:T(8,128)(2,1)}, u32[]{:S(2)}, u32[]{:S(2)}) async-start(bf16[16,32,2048]{2,1,0:T(8,128)(2,1)} %bitcast.181), calls=%async_computation | async-start | bytes 4194304 | tf_op jit(solution)/shard_map/all_to_all | solution.py:125
  115.1 156.9 %reduce-scatter.14.cloned.1.call-start = ((), (), s32[]{:S(2)}) async-start(), calls=%async_computation.8 | async-start | bytes 3342336
  168.0 3.3 copy-start.6
  168.0 3.3 copy-start.23
  171.3 1.2 copy-start.5
  174.5 0.7 copy-start.8
  182.6 162.0 %reduce-scatter.12.cloned.1.call-start = ((), (), s32[]{:S(2)}) async-start(), calls=%async_computation.7 | async-start | bytes 3342336
  205.5 5.2 %copy-start.7 = (bf16[704,256]{1,0:T(8,128)(2,1)S(1)}, bf16[704,256]{1,0:T(8,128)(2,1)}, u32[]{:S(2)}) copy-start(bf16[704,256]{1,0:T(8,128)(2,1)} %get-tuple-element.13) | copy-start | bytes 1081348
  205.5 54.2 %all-to-all-start.2 = ((bf16[16,32,2048]{2,1,0:T(8,128)(2,1)}), bf16[16,32,2048]{2,1,0:T(8,128)(2,1)}, u32[]{:S(2)}, u32[]{:S(2)}) async-start(bf16[16,32,2048]{2,1,0:T(8,128)(2,1)} %bitcast.182), calls=%async_computation.2 | async-start | bytes 4194304 | tf_op jit(solution)/shard_map/all_to_all | solution.py:151
  210.7 217.8 %reduce-scatter.10.cloned.1.call-start = ((), (), s32[]{:S(2)}) async-start(), calls=%async_computation.6 | async-start | bytes 3342336
  219.2 1.0 copy-start.9
  223.5 1.2 collective-permute-start
  263.2 5.6 %copy-start.3 = (bf16[128,2048]{1,0:T(8,128)(2,1)S(1)}, bf16[128,2048]{1,0:T(8,128)(2,1)}, u32[]{:S(2)}) copy-start(bf16[128,2048]{1,0:T(8,128)(2,1)} %param.15) | copy-start | bytes 1572868
  263.2 5.6 %copy-start.17 = (f32[128]{0:T(128)S(1)}, f32[128]{0:T(128)}, u32[]{:S(2)}) copy-start(f32[128]{0:T(128)} %copy-done.16) | copy-start | bytes 1540
  263.2 5.6 %copy-start.20 = (f32[128]{0:T(128)S(1)}, f32[128]{0:T(128)}, u32[]{:S(2)}) copy-start(f32[128]{0:T(128)} %copy-done.19) | copy-start | bytes 1540
Sparse Core Ops, SparseCore 0:
  182.7 78.3 reduce-scatter.13
  264.8 79.8 reduce-scatter.11
  348.3 80.1 reduce-scatter.9
where the time goes:
time: 438 us; the launch traced here: 437 us
  waiting for transfers between devices  229 us (52%)
  local copies, waits for them, and re-layouts  63.4 us (14%)
  blocking collectives  60.9 us (14%)
  other arithmetic  30.6 us (7%)
  matrix products  28.6 us (7%)
  between operations  14.2 us (3%)
  starting transfers between devices  10.2 us (2%)
    unnamed x6, waiting for transfers between devices  153 us
    all_to_all x1, blocking collectives, on_device(): lax.all_to_all(pick_rows(modulated, full_table, tok_dev).reshape(peer_cou...  60.9 us
    all_to_all x1, waiting for transfers between devices, on_device(): lax.all_to_all(pick_rows(scaled, full_table, tok_dev).reshape(peer_count,...  40.5 us
    all_to_all x1, waiting for transfers between devices, on_device(): lax.all_to_all(d_blocks.astype(jnp.bfloat16), 'exp', split_axis=0, concat...  34.5 us
    unnamed x57, local copies, waits for them, and re-layouts  20 us
    scatter x2, local copies, waits for them, and re-layouts, on_device(): full_table.at[jnp.where(is_mine, targets, buffer_rows)]  16.3 us
    gather x2, local copies, waits for them, and re-layouts, pick_rows(): taken_rows = jnp.take(values, jnp.minimum(send_table, tok_dev - 1), axis=0)  9.64 us
  transfers between devices with their start and end apart: 6, of which 5 were waited for; matrix products, arithmetic and copies ran while one was open for 13% of the time, Pallas kernels for 0%

commit v1 on v0

v1 whole, which is shorter than its diff:
```python
import functools

import jax
import jax.numpy as jnp
from jax import lax
from jax.experimental import pallas as pl
from jax.experimental.pallas import tpu as pltpu
from jax.sharding import PartitionSpec as P

EPSILON = 1e-06
MESH = pl.DeviceIdType.MESH
F32 = jnp.float32
BF16 = jnp.bfloat16
SLOT = 32
SIDE = 4
NN = (((1,), (0,)), ((), ()))
NT = (((1,), (1,)), ((), ()))
TN = (((0,), (0,)), ((), ()))


def mm(a, b, dims):
    return lax.dot_general(a, b, dims, preferred_element_type=F32)


def iota(shape, axis):
    return lax.broadcasted_iota(jnp.int32, shape, axis)


def loop(count, body):
    def step(i, carry):
        body(i)
        return carry

    lax.fori_loop(0, count, step, 0)


def layer_kernel(
    nz,
    tok_ref,
    cot_ref,
    step_ref,
    shift_ref,
    scale_ref,
    gate_ref,
    chosen_ref,
    combine_ref,
    wg_hbm,
    wu_hbm,
    wd_hbm,
    dtok_ref,
    dcomb_ref,
    dwg_ref,
    dwu_ref,
    dwd_ref,
    wg,
    wu,
    wd,
    send_a,
    send_b,
    recv_a,
    recv_b,
    rows_in,
    rows_grad,
    normed,
    scale1,
    table,
    inverse,
    pick,
    pick_t,
    place,
    place_t,
    hidden,
    hidden_c,
    gate_f,
    up_f,
    d_gate,
    d_up,
    d_gate_t,
    d_up_t,
    back,
    sib,
    send_c,
    ret,
    inner_s,
    inner_r,
    grads,
    far1,
    near1,
    far2,
    near2,
    w_sem,
    a_send,
    a_recv,
    b_send,
    b_recv,
    fa_send,
    fb_send,
    c_send,
    c_recv,
    s_send,
    s_recv,
    r_send,
    r_recv,
):
    tok_dev, width = tok_ref.shape
    half = wg.shape[0]
    cap = rows_in.shape[0]
    rows_h = half // 2
    rows_q = half // 4
    g = lax.axis_index("grp")
    me = lax.axis_index("exp")
    z = lax.div(me, 2)
    core = lax.rem(me, 2)
    gx = lax.div(g, SIDE)
    gy = lax.rem(g, SIDE)
    sibling = z * 2 + (1 - core)

    def peer(j):
        return lax.rem(z + j, nz)

    def on_z(zz):
        return {"grp": g, "exp": zz * 2 + core}

    on_sib = {"grp": g, "exp": sibling}

    def on_axis(axis, by):
        if axis == 0:
            return {"grp": lax.rem(gx + by, SIDE) * SIDE + gy, "exp": me}
        return {"grp": gx * SIDE + lax.rem(gy + by, SIDE), "exp": me}

    hops = [4, 3, 5, 2, 6, 1, 7] if nz == 8 else list(range(1, nz))

    loads = [
        pltpu.make_async_copy(src, dst, w_sem.at[i])
        for i, (src, dst) in enumerate(((wg_hbm, wg), (wu_hbm, wu), (wd_hbm, wd)))
    ]
    for load in loads:
        load.start()
    barrier = pltpu.get_barrier_semaphore()
    partners = [on_z(peer(j)) for j in hops] + [on_sib]
    partners += [on_axis(axis, by) for axis in (0, 1) for by in (1, SIDE - 1)]
    for partner in partners:
        pl.semaphore_signal(barrier, inc=1, device_id=partner, device_id_type=MESH)

    first = me * tok_dev
    ids = iota((tok_dev, cap), 0) + first
    lane_e = iota((tok_dev, nz), 1)
    mask = jnp.zeros((tok_dev, nz), F32)
    for e in range(nz):
        hit = jnp.sum(
            jnp.where(ids == chosen_ref[e : e + 1, :], 1.0, 0.0), axis=1, keepdims=True
        )
        mask = jnp.where(lane_e == e, hit, mask)
    earlier = (iota((tok_dev, tok_dev), 1) < iota((tok_dev, tok_dev), 0)).astype(F32)
    rank = mm(earlier.astype(BF16), mask.astype(BF16), NN)
    slots = nz * SLOT
    spread = (lax.div(iota((nz, slots), 1), SLOT) == iota((nz, slots), 0)).astype(F32).astype(BF16)
    rank_p = mm(rank.astype(BF16), spread, NN)
    mask_p = mm(mask.astype(BF16), spread, NN)
    want = lax.rem(iota((tok_dev, slots), 1), SLOT).astype(F32)
    pick_f = jnp.where((rank_p == want) & (mask_p > 0.5), 1.0, 0.0)
    pick_t[...] = pick_f.astype(BF16)
    pick[...] = pick_f.T.astype(BF16)

    steps3 = 3 * scale_ref.shape[0]
    onehot = (lax.rem(iota((steps3, tok_dev), 0), scale_ref.shape[0]) == step_ref[...]).astype(F32)
    onehot = onehot.T.astype(BF16)

    def table_rows(ref):
        whole = ref[...]
        hi = whole.astype(BF16)
        rest = whole - hi.astype(F32)
        mid = rest.astype(BF16)
        low = (rest - mid.astype(F32)).astype(BF16)
        return mm(onehot, jnp.concatenate([hi, mid, low], axis=0), NN)

    scale1[...] = 1.0 + table_rows(scale_ref)
    table[...] = table_rows(shift_ref)

    def normalise(i):
        at = pl.ds(pl.multiple_of(i * 16, 16), 16)
        values = tok_ref[at, :].astype(F32)
        centred = values - jnp.mean(values, axis=1, keepdims=True)
        inv = lax.rsqrt(jnp.mean(centred * centred, axis=1, keepdims=True) + EPSILON)
        inverse[at, :] = inv
        norm = centred * inv
        normed[at, :] = norm
        table[at, :] = norm * scale1[at, :] + table[at, :]

    loop(tok_dev // 16, normalise)

    def fill(dst, i):
        at = pl.ds(pl.multiple_of(i * 512, 512), 512)
        dst[:, at] = mm(pick[...], table[:, at].astype(BF16), NN).astype(BF16)

    def slot_of(zz, cc):
        return pl.ds(pl.multiple_of((cc * nz + zz) * SLOT, SLOT), SLOT)

    def block_of(zz):
        return pl.ds(pl.multiple_of(zz * SLOT, SLOT), SLOT)

    def to_peer(src, dst, s_sem, r_sem, j):
        zz = peer(j)
        return pltpu.make_async_remote_copy(
            src_ref=src.at[block_of(zz)],
            dst_ref=dst.at[slot_of(z, core)],
            send_sem=s_sem.at[j],
            recv_sem=r_sem.at[j],
            device_id=on_z(zz),
            device_id_type=MESH,
        )

    def from_peer(dst, s_sem, r_sem, j):
        zz = peer(nz - j)
        return pltpu.make_async_remote_copy(
            src_ref=dst.at[slot_of(zz, core)],
            dst_ref=dst.at[slot_of(zz, core)],
            send_sem=s_sem.at[j],
            recv_sem=r_sem.at[j],
            device_id=on_z(peer(j)),
            device_id_type=MESH,
        )

    def to_sibling(dst, s_sem, r_sem, j):
        zz = peer(nz - j)
        return pltpu.make_async_remote_copy(
            src_ref=dst.at[slot_of(zz, core)],
            dst_ref=dst.at[slot_of(zz, core)],
            send_sem=s_sem.at[j],
            recv_sem=r_sem.at[nz + j],
            device_id=on_sib,
            device_id_type=MESH,
        )

    def from_sibling(dst, s_sem, r_sem, j):
        zz = peer(nz - j)
        return pltpu.make_async_remote_copy(
            src_ref=dst.at[slot_of(zz, 1 - core)],
            dst_ref=dst.at[slot_of(zz, 1 - core)],
            send_sem=s_sem.at[j],
            recv_sem=r_sem.at[nz + j],
            device_id=on_sib,
            device_id_type=MESH,
        )

    loop(width // 512, functools.partial(fill, send_a))
    pl.semaphore_wait(barrier, len(partners))
    for j in hops:
        to_peer(send_a, recv_a, a_send, a_recv, j).start()
    recv_a[slot_of(z, core), :] = send_a[block_of(z), :]
    to_sibling(recv_a, fa_send, a_recv, 0).start()

    table[...] = table_rows(gate_ref)

    def weigh(i):
        at = pl.ds(pl.multiple_of(i * 16, 16), 16)
        table[at, :] = table[at, :] * cot_ref[at, :].astype(F32)

    loop(tok_dev // 16, weigh)
    loop(width // 512, functools.partial(fill, send_b))
    recv_b[slot_of(z, core), :] = send_b[block_of(z), :]
    to_sibling(recv_b, fb_send, b_recv, 0).start()

    row = chosen_ref[pl.ds(z, 1), :]
    diagonal = iota((cap, cap), 0) == iota((cap, cap), 1)
    column = jnp.sum(jnp.where(diagonal, row.astype(F32), 0.0), axis=1, keepdims=True)
    row_f = row.astype(F32)
    owner_row = jnp.floor(row_f * (1.0 / tok_dev))
    owner_col = jnp.floor(column * (1.0 / tok_dev))
    ahead = jnp.where((owner_row == owner_col) & (row_f < column), 1.0, 0.0)
    place_in = jnp.sum(ahead, axis=1, keepdims=True)
    owner_z = jnp.floor(owner_col * 0.5)
    owner_c = owner_col - 2.0 * owner_z
    at_slot = (owner_c * nz + owner_z) * SLOT + place_in
    place_f = jnp.where(
        iota((cap, 2 * slots), 1).astype(F32) == at_slot, 1.0, 0.0
    )
    place[...] = place_f.astype(BF16)
    place_t[...] = place_f.T.astype(BF16)

    for j in hops:
        from_peer(recv_a, a_send, a_recv, j).wait_recv()
        to_sibling(recv_a, fa_send, a_recv, j).start()
        to_peer(send_a, recv_a, a_send, a_recv, j).wait_send()
        to_peer(send_b, recv_b, b_send, b_recv, j).start()
    for j in [0] + hops:
        from_sibling(recv_a, fa_send, a_recv, j).wait_recv()

    def gather(src, dst, i):
        at = pl.ds(pl.multiple_of(i * 512, 512), 512)
        dst[:, at] = mm(place[...], src[:, at], NN).astype(BF16)

    loop(width // 512, functools.partial(gather, recv_a, rows_in))
    for load in loads:
        load.wait()
    weight = combine_ref[pl.ds(z, 1), :]

    def forward(i):
        at = pl.ds(pl.multiple_of(i * rows_q, rows_q), rows_q)
        pre_gate = mm(wg[at, :], rows_in[...], NT)
        pre_up = mm(wu[at, :], rows_in[...], NT)
        sig = 1.0 / (1.0 + jnp.exp(-pre_gate))
        silu = pre_gate * sig
        hid = silu * pre_up
        hidden[at, :] = hid.astype(BF16)
        hidden_c[at, :] = (hid * weight).astype(BF16)
        up_f[at, :] = silu * weight
        gate_f[at, :] = pre_up * sig * (1.0 + pre_gate * (1.0 - sig)) * weight

    loop(4, forward)

    for j in hops:
        from_peer(recv_b, b_send, b_recv, j).wait_recv()
        to_sibling(recv_b, fb_send, b_recv, j).start()
    for j in [0] + hops:
        from_sibling(recv_b, fb_send, b_recv, j).wait_recv()
    loop(width // 512, functools.partial(gather, recv_b, rows_grad))

    def weight_grad(t, left, right):
        def columns(i):
            at = pl.ds(pl.multiple_of(i * 512, 512), 512)
            product = mm(left[...], right[:, at], NN).astype(BF16)
            for k in range(SIDE):
                piece = product[:, k * 128 : (k + 1) * 128]
                grads[2 * t, i * SIDE + k] = piece[:rows_h]
                grads[2 * t + 1, k * SIDE + i] = piece[rows_h:]

        loop(SIDE, columns)

    def ring(t, h):
        n = 2 * t + h
        ia, ib = (gx, gy) if h == 0 else (gy, gx)
        own, other = h, 1 - h

        def copy(src, dst, k, axis, by):
            return pltpu.make_async_remote_copy(
                src_ref=src,
                dst_ref=dst,
                send_sem=r_send.at[n * 12 + k],
                recv_sem=r_recv.at[n * 12 + k],
                device_id=on_axis(axis, by),
                device_id_type=MESH,
            )

        def pair(dest, q):
            return pl.ds(lax.rem(ia + dest, SIDE) * SIDE + 2 * q, 2)

        def sub(dest):
            return ia * SIDE + lax.rem(ib + dest, SIDE)

        one, two = (1, SIDE - 1), SIDE // 2
        first_copies = [
            copy(grads.at[n, pair(two, 0)], far1.at[n, 0], 0, own, one[0]),
            copy(grads.at[n, pair(two, 1)], far1.at[n, 1], 1, own, one[1]),
            copy(grads.at[n, pair(1, 1)], near1.at[n, 0, pl.ds(2, 2)], 2, own, one[0]),
            copy(grads.at[n, pair(3, 0)], near1.at[n, 1, pl.ds(0, 2)], 3, own, one[1]),
            copy(grads.at[n, pair(1, 0)], near1.at[n, 0, pl.ds(0, 2)], 4, own, one[0]),
            copy(grads.at[n, pair(3, 1)], near1.at[n, 1, pl.ds(2, 2)], 5, own, one[1]),
        ]
        top, low = pl.ds(0, rows_q), pl.ds(rows_q, rows_q)
        next_copies = [
            copy(grads.at[n, sub(two), top], far2.at[n, 0], 6, other, one[0]),
            copy(grads.at[n, sub(two), low], far2.at[n, 1], 7, other, one[1]),
            copy(grads.at[n, sub(1), low], near2.at[n, 0, low], 8, other, one[0]),
            copy(grads.at[n, sub(3), top], near2.at[n, 1, top], 9, other, one[1]),
            copy(grads.at[n, sub(1), top], near2.at[n, 0, top], 10, other, one[0]),
            copy(grads.at[n, sub(3), low], near2.at[n, 1, low], 11, other, one[1]),
        ]

        def start1():
            for c in first_copies[:4]:
                c.start()

        def merge1():
            for side, dest in ((0, 1), (1, 3)):
                first_copies[side].wait_recv()
                base = lax.rem(ia + dest, SIDE) * SIDE + 2 * side

                def add(i):
                    grads[n, base + i] = (
                        grads[n, base + i].astype(F32) + far1[n, side, i].astype(F32)
                    ).astype(BF16)

                loop(2, add)
                first_copies[4 + side].start()

        def finish1():
            for c in first_copies[2:]:
                c.wait_recv()
            base = ia * SIDE

            def add(i):
                grads[n, base + i] = (
                    grads[n, base + i].astype(F32)
                    + near1[n, 0, i].astype(F32)
                    + near1[n, 1, i].astype(F32)
                ).astype(BF16)

            loop(SIDE, add)
            for c in next_copies[:4]:
                c.start()

        def merge2():
            for side, dest, part in ((0, 1, top), (1, 3, low)):
                next_copies[side].wait_recv()
                grads[n, sub(dest), part] = (
                    grads[n, sub(dest), part].astype(F32) + far2[n, side].astype(F32)
                ).astype(BF16)
                next_copies[4 + side].start()

        def finish2(out):
            for c in next_copies[2:]:
                c.wait_recv()
            total = (
                grads[n, sub(0)].astype(F32)
                + near2[n, 0].astype(F32)
                + near2[n, 1].astype(F32)
            )
            out[h * rows_h : (h + 1) * rows_h, :] = (total * (1.0 / (SIDE * SIDE))).astype(BF16)

        def drain():
            for c in first_copies + next_copies:
                c.wait_send()

        return start1, merge1, finish1, merge2, finish2, drain

    rings = {(t, h): ring(t, h) for t in range(3) for h in range(2)}

    def run(t, phase, *args):
        for h in range(2):
            rings[t, h][phase](*args)

    weight_grad(0, hidden_c, rows_grad)
    run(0, 0)

    def backward(i):
        at = pl.ds(pl.multiple_of(i * rows_q, rows_q), rows_q)
        raw = mm(wd[at, :], rows_grad[...], NT)
        inner = jnp.sum(hidden[at, :].astype(F32) * raw, axis=0, keepdims=True)
        d_gate[at, :] = (raw * gate_f[at, :]).astype(BF16)
        d_up[at, :] = (raw * up_f[at, :]).astype(BF16)
        return inner

    inner = backward(0)
    for i in range(1, 4):
        inner = inner + backward(i)
    left, right = inner[:, : cap // 2], inner[:, cap // 2 :]
    mine = jnp.where(core == 0, left, right)
    theirs = jnp.where(core == 0, right, left)
    inner_s[...] = jnp.broadcast_to(theirs, inner_s.shape)
    inner_copy = pltpu.make_async_remote_copy(
        src_ref=inner_s,
        dst_ref=inner_r,
        send_sem=s_send.at[0],
        recv_sem=s_recv.at[0],
        device_id=on_sib,
        device_id_type=MESH,
    )
    inner_copy.start()
    d_gate_t[...] = d_gate[...].astype(F32).T.astype(BF16)
    d_up_t[...] = d_up[...].astype(F32).T.astype(BF16)

    def input_grad(i):
        at = pl.ds(pl.multiple_of(i * 512, 512), 512)
        total = mm(d_gate_t[...], wg[:, at], NN) + mm(d_up_t[...], wu[:, at], NN)
        back[:, at] = mm(place_t[...], total.astype(BF16), NN).astype(BF16)

    loop(width // 512, input_grad)
    their_rows = pl.ds(pl.multiple_of((1 - core) * slots, slots), slots)
    sib_copy = pltpu.make_async_remote_copy(
        src_ref=back.at[their_rows],
        dst_ref=sib,
        send_sem=s_send.at[1],
        recv_sem=s_recv.at[1],
        device_id=on_sib,
        device_id_type=MESH,
    )
    sib_copy.start()
    weight_grad(1, d_gate, rows_in)
    run(1, 0)
    run(0, 1)
    sib_copy.wait_recv()

    def add_halves(i):
        at = pl.ds(pl.multiple_of(i * SLOT, SLOT), SLOT)
        here = slot_of(i, core)
        send_c[at, :] = (back[here, :].astype(F32) + sib[at, :].astype(F32)).astype(BF16)

    loop(nz, add_halves)

    def to_owner(j):
        zz = peer(j)
        return pltpu.make_async_remote_copy(
            src_ref=send_c.at[block_of(zz)],
            dst_ref=ret.at[block_of(z)],
            send_sem=c_send.at[j],
            recv_sem=c_recv.at[j],
            device_id=on_z(zz),
            device_id_type=MESH,
        )

    def from_expert(j):
        zz = peer(nz - j)
        return pltpu.make_async_remote_copy(
            src_ref=ret.at[block_of(zz)],
            dst_ref=ret.at[block_of(zz)],
            send_sem=c_send.at[j],
            recv_sem=c_recv.at[j],
            device_id=on_z(peer(j)),
            device_id_type=MESH,
        )

    for j in hops:
        to_owner(j).start()
    ret[block_of(z), :] = send_c[block_of(z), :]
    weight_grad(2, d_up, rows_in)
    run(2, 0)
    inner_copy.wait_recv()
    dcomb_ref[...] = mine + inner_r[0:1, :]
    run(1, 1)
    run(0, 2)
    run(2, 1)
    run(0, 3)
    run(1, 2)
    run(0, 4, dwd_ref)
    run(1, 3)

    for j in hops:
        from_expert(j).wait_recv()

    def spread_back(i):
        at = pl.ds(pl.multiple_of(i * 512, 512), 512)
        table[:, at] = mm(pick_t[...], ret[:, at], NN)

    loop(width // 512, spread_back)

    def token_grad(i):
        at = pl.ds(pl.multiple_of(i * 16, 16), 16)
        norm = normed[at, :]
        d_norm = table[at, :] * scale1[at, :]
        centre = jnp.mean(d_norm, axis=1, keepdims=True)
        along = jnp.mean(d_norm * norm, axis=1, keepdims=True)
        dtok_ref[at, :] = (inverse[at, :] * (d_norm - centre - norm * along)).astype(BF16)

    loop(tok_dev // 16, token_grad)
    run(2, 2)
    run(1, 4, dwg_ref)
    run(2, 3)
    run(2, 4, dwu_ref)

    for j in hops:
        to_peer(send_b, recv_b, b_send, b_recv, j).wait_send()
        to_owner(j).wait_send()
    for j in [0] + hops:
        to_sibling(recv_a, fa_send, a_recv, j).wait_send()
        to_sibling(recv_b, fb_send, b_recv, j).wait_send()
    inner_copy.wait_send()
    sib_copy.wait_send()
    for t in range(3):
        run(t, 5)


def solution(mesh):
    nz = mesh.shape["exp"] // 2

    def on_device(
        tokens, cotangent, timestep, shift_table, scale_table, gate_table, chosen, combine, w_gate, w_up, w_down
    ):
        tok_dev, width = tokens.shape
        half = w_gate.shape[1]
        cap = chosen.shape[2]
        slots = nz * SLOT
        rows_h, rows_q = half // 2, half // 4
        vmem = pl.BlockSpec(memory_space=pltpu.VMEM)
        hbm = pl.BlockSpec(memory_space=pl.ANY)
        dma = pltpu.SemaphoreType.DMA
        outs = pl.pallas_call(
            functools.partial(layer_kernel, nz),
            out_shape=(
                jax.ShapeDtypeStruct((tok_dev, width), BF16),
                jax.ShapeDtypeStruct((1, cap // 2), F32),
                jax.ShapeDtypeStruct((half, 128), BF16),
                jax.ShapeDtypeStruct((half, 128), BF16),
                jax.ShapeDtypeStruct((half, 128), BF16),
            ),
            in_specs=[vmem] * 8 + [hbm] * 3,
            out_specs=(vmem,) * 5,
            scratch_shapes=[
                pltpu.VMEM((half, width), BF16),
                pltpu.VMEM((half, width), BF16),
                pltpu.VMEM((half, width), BF16),
                pltpu.VMEM((slots, width), BF16),
                pltpu.VMEM((slots, width), BF16),
                pltpu.VMEM((2 * slots, width), BF16),
                pltpu.VMEM((2 * slots, width), BF16),
                pltpu.VMEM((cap, width), BF16),
                pltpu.VMEM((cap, width), BF16),
                pltpu.VMEM((tok_dev, width), F32),
                pltpu.VMEM((tok_dev, width), F32),
                pltpu.VMEM((tok_dev, width), F32),
                pltpu.VMEM((tok_dev, 1), F32),
                pltpu.VMEM((slots, tok_dev), BF16),
                pltpu.VMEM((tok_dev, slots), BF16),
                pltpu.VMEM((cap, 2 * slots), BF16),
                pltpu.VMEM((2 * slots, cap), BF16),
                pltpu.VMEM((half, cap), BF16),
                pltpu.VMEM((half, cap), BF16),
                pltpu.VMEM((half, cap), F32),
                pltpu.VMEM((half, cap), F32),
                pltpu.VMEM((half, cap), BF16),
                pltpu.VMEM((half, cap), BF16),
                pltpu.VMEM((cap, half), BF16),
                pltpu.VMEM((cap, half), BF16),

                pltpu.VMEM((2 * slots, width), BF16),
                pltpu.VMEM((slots, width), BF16),
                pltpu.VMEM((slots, width), BF16),
                pltpu.VMEM((slots, width), BF16),
                pltpu.VMEM((8, cap // 2), F32),
                pltpu.VMEM((8, cap // 2), F32),
                pltpu.VMEM((6, SIDE * SIDE, rows_h, 128), BF16),
                pltpu.VMEM((6, 2, 2, rows_h, 128), BF16),
                pltpu.VMEM((6, 2, SIDE, rows_h, 128), BF16),
                pltpu.VMEM((6, 2, rows_q, 128), BF16),
                pltpu.VMEM((6, 2, rows_h, 128), BF16),
                dma((3,)),
                dma((nz,)),
                dma((2 * nz,)),
                dma((nz,)),
                dma((2 * nz,)),
                dma((nz,)),
                dma((nz,)),
                dma((nz,)),
                dma((nz,)),
                dma((2,)),
                dma((2,)),
                dma((72,)),
                dma((72,)),
            ],
            compiler_params=pltpu.CompilerParams(
                collective_id=0, has_side_effects=True, vmem_limit_bytes=60 * 1024 * 1024
            ),
        )(
            tokens,
            cotangent,
            timestep[None, :],
            shift_table,
            scale_table,
            gate_table,
            chosen[0],
            combine[0],
            w_gate[0],
            w_up[0],
            w_down[0],
        )
        d_tokens, d_combine, d_gate, d_up, d_down = outs
        return d_tokens, d_combine[None], d_gate[None], d_up[None], d_down[None]

    in_specs = (
        P(("grp", "exp"), None),
        P(("grp", "exp"), None),
        P(("grp", "exp")),
        P(),
        P(),
        P(),
        P("grp", None, None),
        P("grp", None, None),
        P("exp", None, None),
        P("exp", None, None),
        P("exp", None, None),
    )
    out_specs = (
        P(("grp", "exp"), None),
        P("grp", "exp", None),
        P("exp", None, "grp"),
        P("exp", None, "grp"),
        P("exp", None, "grp"),
    )
    return jax.shard_map(
        on_device, mesh=mesh, in_specs=in_specs, out_specs=out_specs, check_vma=False
    )
```

time: 438 us -> 125 us (0.29)
  waiting for transfers between devices: 229 us -> 0 us
  Pallas kernels: 0 us -> 116 us
  blocking collectives: 60.9 us -> 0 us
  local copies, waits for them, and re-layouts: 63.4 us -> 7.83 us
  other arithmetic: 30.6 us -> 0 us
  matrix products: 28.6 us -> 0 us
  between operations: 14.2 us -> 0.65 us
  starting transfers between devices: 10.2 us -> 0 us
    unnamed x6 -> x0, waiting for transfers between devices: 153 us -> none
    pallas_call x0 -> x1, Pallas kernels: none -> 116 us  [on_device(): pl.pallas_call(functools.partial(layer_kernel, nz), out_shape=(jax.ShapeD...]
    all_to_all x2 -> x0, waiting for transfers between devices: 75 us -> none  [the longest x1 40.5 us: on_device(): lax.all_to_all(pick_rows(scaled, full_table, tok_dev).reshape(peer_count,...]
    all_to_all x1 -> x0, blocking collectives: 60.9 us -> none  [on_device(): lax.all_to_all(pick_rows(modulated, full_table, tok_dev).reshape(peer_cou...]
    dot_general x12 -> x0, matrix products: 28.6 us -> none  [the longest x1 3.82 us: expert_rows(): grad_up = jnp.dot(d_up, rows_in, preferred_element_type=jnp.float32)]
    scatter x3 -> x0, local copies, waits for them, and re-layouts: 21.4 us -> none  [the longest x2 16.3 us: on_device(): full_table.at[jnp.where(is_mine, targets, buffer_rows)]]
    gather x4 -> x0, local copies, waits for them, and re-layouts: 20.2 us -> none  [the longest x2 9.64 us: pick_rows(): taken_rows = jnp.take(values, jnp.minimum(send_table, tok_dev - 1), axis=0)]
    unnamed x57 -> x5, local copies, waits for them, and re-layouts: 20 us -> 7.83 us
  transfers between devices with their start and end apart: 6 -> 0, of which waited for: 5 -> 0; matrix products, arithmetic and copies ran while one was open for 13% -> 0% of each run, Pallas kernels for 0% -> 0%
where the time goes in v1:
time: 125 us
  Pallas kernels  116 us (93%)
  local copies, waits for them, and re-layouts  7.83 us (6%)
    pallas_call x1, Pallas kernels, on_device(): pl.pallas_call(functools.partial(layer_kernel, nz), out_shape=(jax.ShapeD...  116 us
    unnamed x5, local copies, waits for them, and re-layouts  7.83 us

profile of v1, /device:TPU:1, one launch (start us, length us, event | category | flops | bytes accessed | tf_op | source)
XLA Modules:
  0.0 124.7 jit_solution(4524870130693310769)
XLA Ops:
  0.6 116.3 %shard_map.146 = (bf16[128,2048]{1,0:T(8,128)(2,1)}, f32[1,128]{1,0:T(1,128)}, bf16[704,128]{1,0:T(8,128)(2,1)}, bf16[704,128]{1,0:T(8,128)(2,1)}, bf16[704,128]{1,0:T(8,128)(2,1)}) custom-call(bf16[128,2048]{1,0:T(8,128)(2,1)} %tok_ref.1, bf16[128,2048]{1,0:T(8,128)(2,1)} %cot_ref.1, s32[1,128]{1,0:T(1,128)} %bitcast.18, f32[16,2048]{1,0:T(8,128)} %shift_ref.1, ...), custom_call_target="tpu_custom_call" | custom-call | tf_op jit(solution)/shard_map/pallas_call | solution.py:577
  116.9 1.9 %copy.21 = bf16[128,2048]{1,0:T(8,128)(2,1)} copy(bf16[128,2048]{1,0:T(8,128)(2,1)} %get-tuple-element.20) | data formatting | bytes 1048576
  118.8 1.1 copy.22
  119.9 1.6 %copy.23 = bf16[1,704,128]{2,1,0:T(8,128)(2,1)} copy(bf16[1,704,128]{2,1,0:T(8,128)(2,1)} %bitcast.15) | data formatting | bytes 360448
  121.5 1.6 %copy.24 = bf16[1,704,128]{2,1,0:T(8,128)(2,1)} copy(bf16[1,704,128]{2,1,0:T(8,128)(2,1)} %bitcast.14) | data formatting | bytes 360448
  123.1 1.6 %copy.25 = bf16[1,704,128]{2,1,0:T(8,128)(2,1)} copy(bf16[1,704,128]{2,1,0:T(8,128)(2,1)} %bitcast.13) | data formatting | bytes 360448

commit v2 on v1

--- a/solution.py
+++ b/solution.py
@@ -83,7 +83,11 @@
     ret,
     inner_s,
     inner_r,
+    columns_in,
+    line_rows,
+    line_gate,
     grads,
+    parts,
     far1,
     near1,
     far2,
@@ -101,6 +105,8 @@
     s_recv,
     r_send,
     r_recv,
+    l_send,
+    l_recv,
 ):
     tok_dev, width = tok_ref.shape
     half = wg.shape[0]
@@ -138,7 +144,7 @@
         load.start()
     barrier = pltpu.get_barrier_semaphore()
     partners = [on_z(peer(j)) for j in hops] + [on_sib]
-    partners += [on_axis(axis, by) for axis in (0, 1) for by in (1, SIDE - 1)]
+    partners += [on_axis(axis, by) for axis in (0, 1) for by in (1, 2, 3)]
     for partner in partners:
         pl.semaphore_signal(barrier, inc=1, device_id=partner, device_id_type=MESH)
 
@@ -290,7 +296,38 @@
         at = pl.ds(pl.multiple_of(i * 512, 512), 512)
         dst[:, at] = mm(place[...], src[:, at], NN).astype(BF16)
 
-    loop(width // 512, functools.partial(gather, recv_a, rows_in))
+    def gather_in(i):
+        at = pl.ds(pl.multiple_of(i * 512, 512), 512)
+        product = mm(place[...], recv_a[:, at], NN).astype(BF16)
+        rows_in[:, at] = product
+        for k in range(SIDE):
+            columns_in[i, k] = product[:, k * 128 : (k + 1) * 128]
+
+    loop(SIDE, gather_in)
+
+    def along(axis, by):
+        return lax.rem((gx if axis == 0 else gy) + by, SIDE)
+
+    def line_copy(src, dst, k, axis, by):
+        return pltpu.make_async_remote_copy(
+            src_ref=src,
+            dst_ref=dst,
+            send_sem=l_send.at[k],
+            recv_sem=l_recv.at[k],
+            device_id=on_axis(axis, by),
+            device_id_type=MESH,
+        )
+
+    row_copies = []
+    for by in (2, 1, 3):
+        row_copies.append(
+            line_copy(columns_in.at[along(0, by)], line_rows.at[0, by - 1], by - 1, 0, by)
+        )
+        row_copies.append(
+            line_copy(columns_in.at[:, along(1, by)], line_rows.at[1, by - 1], by + 2, 1, by)
+        )
+    for c in row_copies:
+        c.start()
     for load in loads:
         load.wait()
     weight = combine_ref[pl.ds(z, 1), :]
@@ -316,16 +353,27 @@
         from_sibling(recv_b, fb_send, b_recv, j).wait_recv()
     loop(width // 512, functools.partial(gather, recv_b, rows_grad))
 
-    def weight_grad(t, left, right):
-        def columns(i):
-            at = pl.ds(pl.multiple_of(i * 512, 512), 512)
-            product = mm(left[...], right[:, at], NN).astype(BF16)
-            for k in range(SIDE):
-                piece = product[:, k * 128 : (k + 1) * 128]
-                grads[2 * t, i * SIDE + k] = piece[:rows_h]
-                grads[2 * t + 1, k * SIDE + i] = piece[rows_h:]
-
-        loop(SIDE, columns)
+    def down_grad(i):
+        at = pl.ds(pl.multiple_of(i * 512, 512), 512)
+        product = mm(hidden_c[...], rows_grad[:, at], NN).astype(BF16)
+        for k in range(SIDE):
+            piece = product[:, k * 128 : (k + 1) * 128]
+            grads[0, i * SIDE + k] = piece[:rows_h]
+            grads[1, k * SIDE + i] = piece[rows_h:]
+
+    def line_grad(t, h):
+        n = 2 * t + h
+        mine = (d_gate, d_up)[t - 1]
+        here = [columns_in[gx, k] if h == 0 else columns_in[k, gy] for k in range(SIDE)]
+        total = mm(
+            mine[h * rows_h : (h + 1) * rows_h, :], jnp.concatenate(here, axis=1), NN
+        )
+        for r in range(SIDE - 1):
+            rows = jnp.concatenate([line_rows[h, r, k] for k in range(SIDE)], axis=1)
+            total = total + mm(line_gate[t - 1, h, r], rows, NN)
+        total = total.astype(BF16)
+        for k in range(SIDE):
+            parts[n, k] = total[:, k * 128 : (k + 1) * 128]
 
     def ring(t, h):
         n = 2 * t + h
@@ -346,25 +394,27 @@
             return pl.ds(lax.rem(ia + dest, SIDE) * SIDE + 2 * q, 2)
 
         def sub(dest):
-            return ia * SIDE + lax.rem(ib + dest, SIDE)
+            return lax.rem(ib + dest, SIDE)
 
         one, two = (1, SIDE - 1), SIDE // 2
-        first_copies = [
-            copy(grads.at[n, pair(two, 0)], far1.at[n, 0], 0, own, one[0]),
-            copy(grads.at[n, pair(two, 1)], far1.at[n, 1], 1, own, one[1]),
-            copy(grads.at[n, pair(1, 1)], near1.at[n, 0, pl.ds(2, 2)], 2, own, one[0]),
-            copy(grads.at[n, pair(3, 0)], near1.at[n, 1, pl.ds(0, 2)], 3, own, one[1]),
-            copy(grads.at[n, pair(1, 0)], near1.at[n, 0, pl.ds(0, 2)], 4, own, one[0]),
-            copy(grads.at[n, pair(3, 1)], near1.at[n, 1, pl.ds(2, 2)], 5, own, one[1]),
-        ]
+        first_copies = []
+        if t == 0:
+            first_copies = [
+                copy(grads.at[n, pair(two, 0)], far1.at[n, 0], 0, own, one[0]),
+                copy(grads.at[n, pair(two, 1)], far1.at[n, 1], 1, own, one[1]),
+                copy(grads.at[n, pair(1, 1)], near1.at[n, 0, pl.ds(2, 2)], 2, own, one[0]),
+                copy(grads.at[n, pair(3, 0)], near1.at[n, 1, pl.ds(0, 2)], 3, own, one[1]),
+                copy(grads.at[n, pair(1, 0)], near1.at[n, 0, pl.ds(0, 2)], 4, own, one[0]),
+                copy(grads.at[n, pair(3, 1)], near1.at[n, 1, pl.ds(2, 2)], 5, own, one[1]),
+            ]
         top, low = pl.ds(0, rows_q), pl.ds(rows_q, rows_q)
         next_copies = [
-            copy(grads.at[n, sub(two), top], far2.at[n, 0], 6, other, one[0]),
-            copy(grads.at[n, sub(two), low], far2.at[n, 1], 7, other, one[1]),
-            copy(grads.at[n, sub(1), low], near2.at[n, 0, low], 8, other, one[0]),
-            copy(grads.at[n, sub(3), top], near2.at[n, 1, top], 9, other, one[1]),
-            copy(grads.at[n, sub(1), top], near2.at[n, 0, top], 10, other, one[0]),
-            copy(grads.at[n, sub(3), low], near2.at[n, 1, low], 11, other, one[1]),
+            copy(parts.at[n, sub(two), top], far2.at[n, 0], 6, other, one[0]),
+            copy(parts.at[n, sub(two), low], far2.at[n, 1], 7, other, one[1]),
+            copy(parts.at[n, sub(1), low], near2.at[n, 0, low], 8, other, one[0]),
+            copy(parts.at[n, sub(3), top], near2.at[n, 1, top], 9, other, one[1]),
+            copy(parts.at[n, sub(1), top], near2.at[n, 0, top], 10, other, one[0]),
+            copy(parts.at[n, sub(3), low], near2.at[n, 1, low], 11, other, one[1]),
         ]
 
         def start1():
@@ -384,27 +434,30 @@
                 loop(2, add)
                 first_copies[4 + side].start()
 
+        def start2():
+            for c in next_copies[:4]:
+                c.start()
+
         def finish1():
             for c in first_copies[2:]:
                 c.wait_recv()
             base = ia * SIDE
 
             def add(i):
-                grads[n, base + i] = (
+                parts[n, i] = (
                     grads[n, base + i].astype(F32)
                     + near1[n, 0, i].astype(F32)
                     + near1[n, 1, i].astype(F32)
                 ).astype(BF16)
 
             loop(SIDE, add)
-            for c in next_copies[:4]:
-                c.start()
+            start2()
 
         def merge2():
             for side, dest, part in ((0, 1, top), (1, 3, low)):
                 next_copies[side].wait_recv()
-                grads[n, sub(dest), part] = (
-                    grads[n, sub(dest), part].astype(F32) + far2[n, side].astype(F32)
+                parts[n, sub(dest), part] = (
+                    parts[n, sub(dest), part].astype(F32) + far2[n, side].astype(F32)
                 ).astype(BF16)
                 next_copies[4 + side].start()
 
@@ -412,7 +465,7 @@
             for c in next_copies[2:]:
                 c.wait_recv()
             total = (
-                grads[n, sub(0)].astype(F32)
+                parts[n, sub(0)].astype(F32)
                 + near2[n, 0].astype(F32)
                 + near2[n, 1].astype(F32)
             )
@@ -422,16 +475,13 @@
             for c in first_copies + next_copies:
                 c.wait_send()
 
-        return start1, merge1, finish1, merge2, finish2, drain
+        return start1, merge1, finish1, merge2, finish2, drain, start2
 
     rings = {(t, h): ring(t, h) for t in range(3) for h in range(2)}
 
     def run(t, phase, *args):
         for h in range(2):
             rings[t, h][phase](*args)
-
-    weight_grad(0, hidden_c, rows_grad)
-    run(0, 0)
 
     def backward(i):
         at = pl.ds(pl.multiple_of(i * rows_q, rows_q), rows_q)
@@ -444,6 +494,23 @@
     inner = backward(0)
     for i in range(1, 4):
         inner = inner + backward(i)
+    gate_copies = []
+    for t, grad in ((1, d_gate), (2, d_up)):
+        for by in (2, 1, 3):
+            for h in range(2):
+                gate_copies.append(
+                    line_copy(
+                        grad.at[pl.ds(h * rows_h, rows_h)],
+                        line_gate.at[t - 1, h, by - 1],
+                        6 * t + 3 * h + by - 1,
+                        h,
+                        by,
+                    )
+                )
+    for c in gate_copies:
+        c.start()
+    loop(SIDE, down_grad)
+    run(0, 0)
     left, right = inner[:, : cap // 2], inner[:, cap // 2 :]
     mine = jnp.where(core == 0, left, right)
     theirs = jnp.where(core == 0, right, left)
@@ -476,8 +543,6 @@
         device_id_type=MESH,
     )
     sib_copy.start()
-    weight_grad(1, d_gate, rows_in)
-    run(1, 0)
     run(0, 1)
     sib_copy.wait_recv()
 
@@ -513,18 +578,20 @@
     for j in hops:
         to_owner(j).start()
     ret[block_of(z), :] = send_c[block_of(z), :]
-    weight_grad(2, d_up, rows_in)
-    run(2, 0)
     inner_copy.wait_recv()
     dcomb_ref[...] = mine + inner_r[0:1, :]
-    run(1, 1)
+    for c in row_copies:
+        c.wait_recv()
+    for t in (1, 2):
+        for c in gate_copies[6 * (t - 1) : 6 * t]:
+            c.wait_recv()
+        for h in range(2):
+            line_grad(t, h)
+            rings[t, h][6]()
     run(0, 2)
-    run(2, 1)
+    run(1, 3)
+    run(2, 3)
     run(0, 3)
-    run(1, 2)
-    run(0, 4, dwd_ref)
-    run(1, 3)
-
     for j in hops:
         from_expert(j).wait_recv()
 
@@ -543,10 +610,9 @@
         dtok_ref[at, :] = (inverse[at, :] * (d_norm - centre - norm * along)).astype(BF16)
 
     loop(tok_dev // 16, token_grad)
-    run(2, 2)
     run(1, 4, dwg_ref)
-    run(2, 3)
     run(2, 4, dwu_ref)
+    run(0, 4, dwd_ref)
 
     for j in hops:
         to_peer(send_b, recv_b, b_send, b_recv, j).wait_send()
@@ -554,10 +620,24 @@
     for j in [0] + hops:
         to_sibling(recv_a, fa_send, a_recv, j).wait_send()
         to_sibling(recv_b, fb_send, b_recv, j).wait_send()
+    for c in row_copies + gate_copies:
+        c.wait_send()
     inner_copy.wait_send()
     sib_copy.wait_send()
     for t in range(3):
         run(t, 5)
+
+
+def copy_kernel(*refs):
+    count = len(refs) // 2
+    sems = refs[-1]
+    copies = [
+        pltpu.make_async_copy(refs[i], refs[count + i], sems.at[i]) for i in range(count)
+    ]
+    for c in copies:
+        c.start()
+    for c in copies:
+        c.wait()
 
 
 def solution(mesh):
@@ -618,9 +698,13 @@
                 pltpu.VMEM((slots, width), BF16),
                 pltpu.VMEM((8, cap // 2), F32),
                 pltpu.VMEM((8, cap // 2), F32),
-                pltpu.VMEM((6, SIDE * SIDE, rows_h, 128), BF16),
-                pltpu.VMEM((6, 2, 2, rows_h, 128), BF16),
-                pltpu.VMEM((6, 2, SIDE, rows_h, 128), BF16),
+                pltpu.VMEM((SIDE, SIDE, cap, 128), BF16),
+                pltpu.VMEM((2, SIDE - 1, SIDE, cap, 128), BF16),
+                pltpu.VMEM((2, 2, SIDE - 1, rows_h, cap), BF16),
+                pltpu.VMEM((2, SIDE * SIDE, rows_h, 128), BF16),
+                pltpu.VMEM((6, SIDE, rows_h, 128), BF16),
+                pltpu.VMEM((2, 2, 2, rows_h, 128), BF16),
+                pltpu.VMEM((2, 2, SIDE, rows_h, 128), BF16),
                 pltpu.VMEM((6, 2, rows_q, 128), BF16),
                 pltpu.VMEM((6, 2, rows_h, 128), BF16),
                 dma((3,)),
@@ -636,6 +720,8 @@
                 dma((2,)),
                 dma((72,)),
                 dma((72,)),
+                dma((18,)),
+                dma((18,)),
             ],
             compiler_params=pltpu.CompilerParams(
                 collective_id=0, has_side_effects=True, vmem_limit_bytes=60 * 1024 * 1024
@@ -653,6 +739,13 @@
             w_up[0],
             w_down[0],
         )
+        outs = pl.pallas_call(
+            copy_kernel,
+            out_shape=tuple(jax.ShapeDtypeStruct(o.shape, o.dtype) for o in outs),
+            in_specs=[hbm] * 5,
+            out_specs=(hbm,) * 5,
+            scratch_shapes=[dma((5,))],
+        )(*outs)
         d_tokens, d_combine, d_gate, d_up, d_down = outs
         return d_tokens, d_combine[None], d_gate[None], d_up[None], d_down[None]
 

time: 125 us -> 149 us (1.19)
  Pallas kernels: 116 us -> 149 us
  local copies, waits for them, and re-layouts: 7.83 us -> 0 us
    pallas_call x0 -> x1, Pallas kernels: none -> 33.4 us  [on_device(): pl.pallas_call(copy_kernel, out_shape=tuple((jax.ShapeDtypeStruct(o.shape...]
    unnamed x5 -> x0, local copies, waits for them, and re-layouts: 7.83 us -> none
where the time goes in v2:
time: 149 us
  Pallas kernels  149 us (100%)
    pallas_call x1, Pallas kernels, on_device(): pl.pallas_call(functools.partial(layer_kernel, nz), out_shape=(jax.ShapeD...  115 us
    pallas_call x1, Pallas kernels, on_device(): pl.pallas_call(copy_kernel, out_shape=tuple((jax.ShapeDtypeStruct(o.shape...  33.4 us

profile of v2, /device:TPU:1, one launch (start us, length us, event | category | flops | bytes accessed | tf_op | source)
XLA Modules:
  0.0 149.3 jit_solution(3629443456852011360)
XLA Ops:
  0.6 115.3 %shard_map.146 = (bf16[128,2048]{1,0:T(8,128)(2,1)}, f32[1,128]{1,0:T(1,128)}, bf16[704,128]{1,0:T(8,128)(2,1)}, bf16[704,128]{1,0:T(8,128)(2,1)}, bf16[704,128]{1,0:T(8,128)(2,1)}) custom-call(bf16[128,2048]{1,0:T(8,128)(2,1)} %tok_ref.1, bf16[128,2048]{1,0:T(8,128)(2,1)} %cot_ref.1, s32[1,128]{1,0:T(1,128)} %bitcast.15, f32[16,2048]{1,0:T(8,128)} %shift_ref.1, ...), custom_call_target="tpu_custom_call" | custom-call | tf_op jit(solution)/shard_map/pallas_call | solution.py:657
  115.9 33.4 %shard_map.147 = (bf16[128,2048]{1,0:T(8,128)(2,1)}, f32[1,128]{1,0:T(1,128)}, bf16[704,128]{1,0:T(8,128)(2,1)}, bf16[704,128]{1,0:T(8,128)(2,1)}, bf16[704,128]{1,0:T(8,128)(2,1)}) custom-call(bf16[128,2048]{1,0:T(8,128)(2,1)} %get-tuple-element.15.refs_0_, f32[1,128]{1,0:T(1,128)} %get-tuple-element.16.refs_1_, ...), custom_call_target="tpu_custom_call" | custom-call | tf_op jit(solution)/shard_map/pallas_call | solution.py:742

commit v3 on v2

--- a/solution.py
+++ b/solution.py
@@ -13,6 +13,7 @@
 BF16 = jnp.bfloat16
 SLOT = 32
 SIDE = 4
+CHUNKS = 2
 NN = (((1,), (0,)), ((), ()))
 NT = (((1,), (1,)), ((), ()))
 TN = (((0,), (0,)), ((), ()))
@@ -134,7 +135,7 @@
             return {"grp": lax.rem(gx + by, SIDE) * SIDE + gy, "exp": me}
         return {"grp": gx * SIDE + lax.rem(gy + by, SIDE), "exp": me}
 
-    hops = [4, 3, 5, 2, 6, 1, 7] if nz == 8 else list(range(1, nz))
+    hops = [1, 7, 2, 6, 3, 5, 4] if nz == 8 else list(range(1, nz))
 
     loads = [
         pltpu.make_async_copy(src, dst, w_sem.at[i])
@@ -509,8 +510,6 @@
                 )
     for c in gate_copies:
         c.start()
-    loop(SIDE, down_grad)
-    run(0, 0)
     left, right = inner[:, : cap // 2], inner[:, cap // 2 :]
     mine = jnp.where(core == 0, left, right)
     theirs = jnp.where(core == 0, right, left)
@@ -527,61 +526,73 @@
     d_gate_t[...] = d_gate[...].astype(F32).T.astype(BF16)
     d_up_t[...] = d_up[...].astype(F32).T.astype(BF16)
 
+    chunk = width // CHUNKS
+    own_rows = pl.ds(pl.multiple_of(core * slots, slots), slots)
+    their_rows = pl.ds(pl.multiple_of((1 - core) * slots, slots), slots)
+
+    def columns(i):
+        return pl.ds(i * chunk, chunk)
+
+    sib_copies = [
+        pltpu.make_async_remote_copy(
+            src_ref=back.at[their_rows, columns(i)],
+            dst_ref=sib.at[:, columns(i)],
+            send_sem=s_send.at[1 + i],
+            recv_sem=s_recv.at[1 + i],
+            device_id=on_sib,
+            device_id_type=MESH,
+        )
+        for i in range(CHUNKS)
+    ]
+
+    def to_owner(j, i):
+        zz = peer(j)
+        return pltpu.make_async_remote_copy(
+            src_ref=send_c.at[block_of(zz), columns(i)],
+            dst_ref=ret.at[block_of(z), columns(i)],
+            send_sem=c_send.at[j * CHUNKS + i],
+            recv_sem=c_recv.at[j * CHUNKS + i],
+            device_id=on_z(zz),
+            device_id_type=MESH,
+        )
+
+    def from_expert(j, i):
+        zz = peer(nz - j)
+        return pltpu.make_async_remote_copy(
+            src_ref=ret.at[block_of(zz), columns(i)],
+            dst_ref=ret.at[block_of(zz), columns(i)],
+            send_sem=c_send.at[j * CHUNKS + i],
+            recv_sem=c_recv.at[j * CHUNKS + i],
+            device_id=on_z(peer(j)),
+            device_id_type=MESH,
+        )
+
     def input_grad(i):
-        at = pl.ds(pl.multiple_of(i * 512, 512), 512)
+        at = columns(i)
         total = mm(d_gate_t[...], wg[:, at], NN) + mm(d_up_t[...], wu[:, at], NN)
         back[:, at] = mm(place_t[...], total.astype(BF16), NN).astype(BF16)
-
-    loop(width // 512, input_grad)
-    their_rows = pl.ds(pl.multiple_of((1 - core) * slots, slots), slots)
-    sib_copy = pltpu.make_async_remote_copy(
-        src_ref=back.at[their_rows],
-        dst_ref=sib,
-        send_sem=s_send.at[1],
-        recv_sem=s_recv.at[1],
-        device_id=on_sib,
-        device_id_type=MESH,
-    )
-    sib_copy.start()
-    run(0, 1)
-    sib_copy.wait_recv()
-
-    def add_halves(i):
-        at = pl.ds(pl.multiple_of(i * SLOT, SLOT), SLOT)
-        here = slot_of(i, core)
-        send_c[at, :] = (back[here, :].astype(F32) + sib[at, :].astype(F32)).astype(BF16)
-
-    loop(nz, add_halves)
-
-    def to_owner(j):
-        zz = peer(j)
-        return pltpu.make_async_remote_copy(
-            src_ref=send_c.at[block_of(zz)],
-            dst_ref=ret.at[block_of(z)],
-            send_sem=c_send.at[j],
-            recv_sem=c_recv.at[j],
-            device_id=on_z(zz),
-            device_id_type=MESH,
-        )
-
-    def from_expert(j):
-        zz = peer(nz - j)
-        return pltpu.make_async_remote_copy(
-            src_ref=ret.at[block_of(zz)],
-            dst_ref=ret.at[block_of(zz)],
-            send_sem=c_send.at[j],
-            recv_sem=c_recv.at[j],
-            device_id=on_z(peer(j)),
-            device_id_type=MESH,
-        )
-
-    for j in hops:
-        to_owner(j).start()
-    ret[block_of(z), :] = send_c[block_of(z), :]
+        sib_copies[i].start()
+
+    def send_home(i):
+        at = columns(i)
+        sib_copies[i].wait_recv()
+        send_c[:, at] = (back[own_rows, at].astype(F32) + sib[:, at].astype(F32)).astype(BF16)
+        for j in hops:
+            to_owner(j, i).start()
+        ret[block_of(z), at] = send_c[block_of(z), at]
+
+    for i in range(CHUNKS):
+        input_grad(i)
+        if i:
+            send_home(i - 1)
+    loop(SIDE, down_grad)
+    run(0, 0)
+    send_home(CHUNKS - 1)
     inner_copy.wait_recv()
     dcomb_ref[...] = mine + inner_r[0:1, :]
     for c in row_copies:
         c.wait_recv()
+    run(0, 1)
     for t in (1, 2):
         for c in gate_copies[6 * (t - 1) : 6 * t]:
             c.wait_recv()
@@ -593,7 +604,8 @@
     run(2, 3)
     run(0, 3)
     for j in hops:
-        from_expert(j).wait_recv()
+        for i in range(CHUNKS):
+            from_expert(j, i).wait_recv()
 
     def spread_back(i):
         at = pl.ds(pl.multiple_of(i * 512, 512), 512)
@@ -616,28 +628,24 @@
 
     for j in hops:
         to_peer(send_b, recv_b, b_send, b_recv, j).wait_send()
-        to_owner(j).wait_send()
+        for i in range(CHUNKS):
+            to_owner(j, i).wait_send()
     for j in [0] + hops:
         to_sibling(recv_a, fa_send, a_recv, j).wait_send()
         to_sibling(recv_b, fb_send, b_recv, j).wait_send()
     for c in row_copies + gate_copies:
         c.wait_send()
     inner_copy.wait_send()
-    sib_copy.wait_send()
+    for c in sib_copies:
+        c.wait_send()
     for t in range(3):
         run(t, 5)
 
 
 def copy_kernel(*refs):
     count = len(refs) // 2
-    sems = refs[-1]
-    copies = [
-        pltpu.make_async_copy(refs[i], refs[count + i], sems.at[i]) for i in range(count)
-    ]
-    for c in copies:
-        c.start()
-    for c in copies:
-        c.wait()
+    for i in range(count):
+        refs[count + i][...] = refs[i][...]
 
 
 def solution(mesh):
@@ -714,10 +722,10 @@
                 dma((2 * nz,)),
                 dma((nz,)),
                 dma((nz,)),
-                dma((nz,)),
-                dma((nz,)),
-                dma((2,)),
-                dma((2,)),
+                dma((nz * CHUNKS,)),
+                dma((nz * CHUNKS,)),
+                dma((1 + CHUNKS,)),
+                dma((1 + CHUNKS,)),
                 dma((72,)),
                 dma((72,)),
                 dma((18,)),
@@ -742,9 +750,8 @@
         outs = pl.pallas_call(
             copy_kernel,
             out_shape=tuple(jax.ShapeDtypeStruct(o.shape, o.dtype) for o in outs),
-            in_specs=[hbm] * 5,
-            out_specs=(hbm,) * 5,
-            scratch_shapes=[dma((5,))],
+            in_specs=[vmem] * 5,
+            out_specs=(vmem,) * 5,
         )(*outs)
         d_tokens, d_combine, d_gate, d_up, d_down = outs
         return d_tokens, d_combine[None], d_gate[None], d_up[None], d_down[None]

time: 149 us -> 108 us (0.72)
  Pallas kernels: 149 us -> 108 us
    pallas_call x1, Pallas kernels: 33.4 us -> 2.21 us  [on_device(): pl.pallas_call(copy_kernel, out_shape=tuple((jax.ShapeDtypeStruct(o.shape...]
    pallas_call x1, Pallas kernels: 115 us -> 105 us  [on_device(): pl.pallas_call(functools.partial(layer_kernel, nz), out_shape=(jax.ShapeD...]
where the time goes in v3:
time: 108 us
  Pallas kernels  108 us (100%)
    pallas_call x1, Pallas kernels, on_device(): pl.pallas_call(functools.partial(layer_kernel, nz), out_shape=(jax.ShapeD...  105 us
    pallas_call x1, Pallas kernels, on_device(): pl.pallas_call(copy_kernel, out_shape=tuple((jax.ShapeDtypeStruct(o.shape...  2.21 us

profile of v3, /device:TPU:1, one launch (start us, length us, event | category | flops | bytes accessed | tf_op | source)
XLA Modules:
  0.0 108.2 jit_solution(8907865942081931899)
XLA Ops:
  0.6 105.3 %shard_map.146 = (bf16[128,2048]{1,0:T(8,128)(2,1)}, f32[1,128]{1,0:T(1,128)}, bf16[704,128]{1,0:T(8,128)(2,1)}, bf16[704,128]{1,0:T(8,128)(2,1)}, bf16[704,128]{1,0:T(8,128)(2,1)}) custom-call(bf16[128,2048]{1,0:T(8,128)(2,1)} %tok_ref.1, bf16[128,2048]{1,0:T(8,128)(2,1)} %cot_ref.1, s32[1,128]{1,0:T(1,128)} %bitcast.15, f32[16,2048]{1,0:T(8,128)} %shift_ref.1, ...), custom_call_target="tpu_custom_call" | custom-call | tf_op jit(solution)/shard_map/pallas_call | solution.py:665
  105.9 2.2 %shard_map.147 = (bf16[128,2048]{1,0:T(8,128)(2,1)}, f32[1,128]{1,0:T(1,128)}, bf16[704,128]{1,0:T(8,128)(2,1)}, bf16[704,128]{1,0:T(8,128)(2,1)}, bf16[704,128]{1,0:T(8,128)(2,1)}) custom-call(bf16[128,2048]{1,0:T(8,128)(2,1)} %get-tuple-element.15.refs_0_, f32[1,128]{1,0:T(1,128)} %get-tuple-element.16.refs_1_, ...), custom_call_target="tpu_custom_call" | custom-call | tf_op jit(solution)/shard_map/pallas_call | solution.py:750

commit v4 on v3

--- a/solution.py
+++ b/solution.py
@@ -14,6 +14,7 @@
 SLOT = 32
 SIDE = 4
 CHUNKS = 2
+ORDER = (2, 1, 3, 0)
 NN = (((1,), (0,)), ((), ()))
 NT = (((1,), (1,)), ((), ()))
 TN = (((0,), (0,)), ((), ()))
@@ -74,6 +75,7 @@
     hidden_c,
     gate_f,
     up_f,
+    raw,
     d_gate,
     d_up,
     d_gate_t,
@@ -206,46 +208,56 @@
     def block_of(zz):
         return pl.ds(pl.multiple_of(zz * SLOT, SLOT), SLOT)
 
-    def to_peer(src, dst, s_sem, r_sem, j):
+    def quarter(s):
+        at = lax.rem(gx + ORDER[s], SIDE) * (width // SIDE)
+        return pl.ds(pl.multiple_of(at, width // SIDE), width // SIDE)
+
+    def part(ref, rows, s):
+        return ref.at[rows] if s is None else ref.at[rows, quarter(s)]
+
+    def sem(j, s):
+        return j if s is None else j * SIDE + s
+
+    def to_peer(src, dst, s_sem, r_sem, j, s=None):
         zz = peer(j)
         return pltpu.make_async_remote_copy(
-            src_ref=src.at[block_of(zz)],
-            dst_ref=dst.at[slot_of(z, core)],
-            send_sem=s_sem.at[j],
-            recv_sem=r_sem.at[j],
+            src_ref=part(src, block_of(zz), s),
+            dst_ref=part(dst, slot_of(z, core), s),
+            send_sem=s_sem.at[sem(j, s)],
+            recv_sem=r_sem.at[sem(j, s)],
             device_id=on_z(zz),
             device_id_type=MESH,
         )
 
-    def from_peer(dst, s_sem, r_sem, j):
+    def from_peer(dst, s_sem, r_sem, j, s=None):
         zz = peer(nz - j)
         return pltpu.make_async_remote_copy(
-            src_ref=dst.at[slot_of(zz, core)],
-            dst_ref=dst.at[slot_of(zz, core)],
-            send_sem=s_sem.at[j],
-            recv_sem=r_sem.at[j],
+            src_ref=part(dst, slot_of(zz, core), s),
+            dst_ref=part(dst, slot_of(zz, core), s),
+            send_sem=s_sem.at[sem(j, s)],
+            recv_sem=r_sem.at[sem(j, s)],
             device_id=on_z(peer(j)),
             device_id_type=MESH,
         )
 
-    def to_sibling(dst, s_sem, r_sem, j):
+    def to_sibling(dst, s_sem, r_sem, j, s=None):
         zz = peer(nz - j)
         return pltpu.make_async_remote_copy(
-            src_ref=dst.at[slot_of(zz, core)],
-            dst_ref=dst.at[slot_of(zz, core)],
-            send_sem=s_sem.at[j],
-            recv_sem=r_sem.at[nz + j],
+            src_ref=part(dst, slot_of(zz, core), s),
+            dst_ref=part(dst, slot_of(zz, core), s),
+            send_sem=s_sem.at[sem(j, s)],
+            recv_sem=r_sem.at[sem(nz + j, s)],
             device_id=on_sib,
             device_id_type=MESH,
         )
 
-    def from_sibling(dst, s_sem, r_sem, j):
+    def from_sibling(dst, s_sem, r_sem, j, s=None):
         zz = peer(nz - j)
         return pltpu.make_async_remote_copy(
-            src_ref=dst.at[slot_of(zz, 1 - core)],
-            dst_ref=dst.at[slot_of(zz, 1 - core)],
-            send_sem=s_sem.at[j],
-            recv_sem=r_sem.at[nz + j],
+            src_ref=part(dst, slot_of(zz, 1 - core), s),
+            dst_ref=part(dst, slot_of(zz, 1 - core), s),
+            send_sem=s_sem.at[sem(j, s)],
+            recv_sem=r_sem.at[sem(nz + j, s)],
             device_id=on_sib,
             device_id_type=MESH,
         )
@@ -266,7 +278,8 @@
     loop(tok_dev // 16, weigh)
     loop(width // 512, functools.partial(fill, send_b))
     recv_b[slot_of(z, core), :] = send_b[block_of(z), :]
-    to_sibling(recv_b, fb_send, b_recv, 0).start()
+    for s in range(SIDE):
+        to_sibling(recv_b, fb_send, b_recv, 0, s).start()
 
     row = chosen_ref[pl.ds(z, 1), :]
     diagonal = iota((cap, cap), 0) == iota((cap, cap), 1)
@@ -289,13 +302,12 @@
         from_peer(recv_a, a_send, a_recv, j).wait_recv()
         to_sibling(recv_a, fa_send, a_recv, j).start()
         to_peer(send_a, recv_a, a_send, a_recv, j).wait_send()
-        to_peer(send_b, recv_b, b_send, b_recv, j).start()
+        to_peer(send_b, recv_b, b_send, b_recv, j, 0).start()
+    for s in range(1, SIDE):
+        for j in hops:
+            to_peer(send_b, recv_b, b_send, b_recv, j, s).start()
     for j in [0] + hops:
         from_sibling(recv_a, fa_send, a_recv, j).wait_recv()
-
-    def gather(src, dst, i):
-        at = pl.ds(pl.multiple_of(i * 512, 512), 512)
-        dst[:, at] = mm(place[...], src[:, at], NN).astype(BF16)
 
     def gather_in(i):
         at = pl.ds(pl.multiple_of(i * 512, 512), 512)
@@ -347,20 +359,15 @@
 
     loop(4, forward)
 
-    for j in hops:
-        from_peer(recv_b, b_send, b_recv, j).wait_recv()
-        to_sibling(recv_b, fb_send, b_recv, j).start()
-    for j in [0] + hops:
-        from_sibling(recv_b, fb_send, b_recv, j).wait_recv()
-    loop(width // 512, functools.partial(gather, recv_b, rows_grad))
-
-    def down_grad(i):
-        at = pl.ds(pl.multiple_of(i * 512, 512), 512)
-        product = mm(hidden_c[...], rows_grad[:, at], NN).astype(BF16)
+    def down_grad(s):
+        product = mm(hidden_c[...], rows_grad[:, quarter(s)], NN).astype(BF16)
         for k in range(SIDE):
             piece = product[:, k * 128 : (k + 1) * 128]
-            grads[0, i * SIDE + k] = piece[:rows_h]
-            grads[1, k * SIDE + i] = piece[rows_h:]
+            grads[0, s * SIDE + k] = piece[:rows_h]
+            grads[1, k * SIDE + s] = piece[rows_h:]
+        ready = {0: ((0, 0), (0, 1)), 1: ((0, 2), (1, 0), (1, 3)), 2: ((0, 3),), 3: ((1, 1), (1, 2))}
+        for h, k in ready[s]:
+            rings[0, h][0][k].start()
 
     def line_grad(t, h):
         n = 2 * t + h
@@ -391,11 +398,14 @@
                 device_id_type=MESH,
             )
 
+        def block(dest):
+            return (ORDER.index(dest) if h == 0 else lax.rem(ia + dest, SIDE)) * SIDE
+
         def pair(dest, q):
-            return pl.ds(lax.rem(ia + dest, SIDE) * SIDE + 2 * q, 2)
+            return pl.ds(block(dest) + 2 * q, 2)
 
         def sub(dest):
-            return lax.rem(ib + dest, SIDE)
+            return ORDER.index(dest) if t == 0 and h == 1 else lax.rem(ib + dest, SIDE)
 
         one, two = (1, SIDE - 1), SIDE // 2
         first_copies = []
@@ -418,14 +428,10 @@
             copy(parts.at[n, sub(3), low], near2.at[n, 1, low], 11, other, one[1]),
         ]
 
-        def start1():
-            for c in first_copies[:4]:
-                c.start()
-
         def merge1():
             for side, dest in ((0, 1), (1, 3)):
                 first_copies[side].wait_recv()
-                base = lax.rem(ia + dest, SIDE) * SIDE + 2 * side
+                base = block(dest) + 2 * side
 
                 def add(i):
                     grads[n, base + i] = (
@@ -442,7 +448,7 @@
         def finish1():
             for c in first_copies[2:]:
                 c.wait_recv()
-            base = ia * SIDE
+            base = block(0)
 
             def add(i):
                 parts[n, i] = (
@@ -476,7 +482,7 @@
             for c in first_copies + next_copies:
                 c.wait_send()
 
-        return start1, merge1, finish1, merge2, finish2, drain, start2
+        return first_copies, merge1, finish1, merge2, finish2, drain, start2
 
     rings = {(t, h): ring(t, h) for t in range(3) for h in range(2)}
 
@@ -484,13 +490,28 @@
         for h in range(2):
             rings[t, h][phase](*args)
 
+    def raw_sum(s, i):
+        at = pl.ds(pl.multiple_of(i * rows_q, rows_q), rows_q)
+        product = mm(wd[at, quarter(s)], rows_grad[:, quarter(s)], NT)
+        raw[at, :] = product if s == 0 else raw[at, :] + product
+
+    for s in range(SIDE):
+        for j in hops:
+            from_peer(recv_b, b_send, b_recv, j, s).wait_recv()
+            to_sibling(recv_b, fb_send, b_recv, j, s).start()
+        for j in [0] + hops:
+            from_sibling(recv_b, fb_send, b_recv, j, s).wait_recv()
+        rows_grad[:, quarter(s)] = mm(place[...], recv_b[:, quarter(s)], NN).astype(BF16)
+        loop(4, functools.partial(raw_sum, s))
+        if s < SIDE - 1:
+            down_grad(s)
+
     def backward(i):
-        at = pl.ds(pl.multiple_of(i * rows_q, rows_q), rows_q)
-        raw = mm(wd[at, :], rows_grad[...], NT)
-        inner = jnp.sum(hidden[at, :].astype(F32) * raw, axis=0, keepdims=True)
-        d_gate[at, :] = (raw * gate_f[at, :]).astype(BF16)
-        d_up[at, :] = (raw * up_f[at, :]).astype(BF16)
-        return inner
+        at = pl.ds(i * rows_q, rows_q)
+        value = raw[at, :]
+        d_gate[at, :] = (value * gate_f[at, :]).astype(BF16)
+        d_up[at, :] = (value * up_f[at, :]).astype(BF16)
+        return jnp.sum(hidden[at, :].astype(F32) * value, axis=0, keepdims=True)
 
     inner = backward(0)
     for i in range(1, 4):
@@ -585,8 +606,7 @@
         input_grad(i)
         if i:
             send_home(i - 1)
-    loop(SIDE, down_grad)
-    run(0, 0)
+    down_grad(SIDE - 1)
     send_home(CHUNKS - 1)
     inner_copy.wait_recv()
     dcomb_ref[...] = mine + inner_r[0:1, :]
@@ -627,12 +647,14 @@
     run(0, 4, dwd_ref)
 
     for j in hops:
-        to_peer(send_b, recv_b, b_send, b_recv, j).wait_send()
+        for s in range(SIDE):
+            to_peer(send_b, recv_b, b_send, b_recv, j, s).wait_send()
         for i in range(CHUNKS):
             to_owner(j, i).wait_send()
     for j in [0] + hops:
         to_sibling(recv_a, fa_send, a_recv, j).wait_send()
-        to_sibling(recv_b, fb_send, b_recv, j).wait_send()
+        for s in range(SIDE):
+            to_sibling(recv_b, fb_send, b_recv, j, s).wait_send()
     for c in row_copies + gate_copies:
         c.wait_send()
     inner_copy.wait_send()
@@ -695,6 +717,7 @@
                 pltpu.VMEM((half, cap), BF16),
                 pltpu.VMEM((half, cap), F32),
                 pltpu.VMEM((half, cap), F32),
+                pltpu.VMEM((half, cap), F32),
                 pltpu.VMEM((half, cap), BF16),
                 pltpu.VMEM((half, cap), BF16),
                 pltpu.VMEM((cap, half), BF16),
@@ -718,10 +741,10 @@
                 dma((3,)),
                 dma((nz,)),
                 dma((2 * nz,)),
+                dma((nz * SIDE,)),
+                dma((2 * nz * SIDE,)),
                 dma((nz,)),
-                dma((2 * nz,)),
-                dma((nz,)),
-                dma((nz,)),
+                dma((nz * SIDE,)),
                 dma((nz * CHUNKS,)),
                 dma((nz * CHUNKS,)),
                 dma((1 + CHUNKS,)),

time: 108 us -> 105 us (0.972)
  Pallas kernels: 108 us -> 104 us
    pallas_call x1, Pallas kernels: 105 us -> 102 us  [on_device(): pl.pallas_call(functools.partial(layer_kernel, nz), out_shape=(jax.ShapeD...]
where the time goes in v4:
time: 105 us
  Pallas kernels  104 us (99%)
    pallas_call x1, Pallas kernels, on_device(): pl.pallas_call(functools.partial(layer_kernel, nz), out_shape=(jax.ShapeD...  102 us
    pallas_call x1, Pallas kernels, on_device(): pl.pallas_call(copy_kernel, out_shape=tuple((jax.ShapeDtypeStruct(o.shape...  2.21 us

profile of v4, /device:TPU:1, one launch (start us, length us, event | category | flops | bytes accessed | tf_op | source)
XLA Modules:
  0.0 104.7 jit_solution(5628768272731737159)
XLA Ops:
  0.6 101.8 %shard_map.146 = (bf16[128,2048]{1,0:T(8,128)(2,1)}, f32[1,128]{1,0:T(1,128)}, bf16[704,128]{1,0:T(8,128)(2,1)}, bf16[704,128]{1,0:T(8,128)(2,1)}, bf16[704,128]{1,0:T(8,128)(2,1)}) custom-call(bf16[128,2048]{1,0:T(8,128)(2,1)} %tok_ref.1, bf16[128,2048]{1,0:T(8,128)(2,1)} %cot_ref.1, s32[1,128]{1,0:T(1,128)} %bitcast.15, f32[16,2048]{1,0:T(8,128)} %shift_ref.1, ...), custom_call_target="tpu_custom_call" | custom-call | tf_op jit(solution)/shard_map/pallas_call | solution.py:687
  102.5 2.2 %shard_map.147 = (bf16[128,2048]{1,0:T(8,128)(2,1)}, f32[1,128]{1,0:T(1,128)}, bf16[704,128]{1,0:T(8,128)(2,1)}, bf16[704,128]{1,0:T(8,128)(2,1)}, bf16[704,128]{1,0:T(8,128)(2,1)}) custom-call(bf16[128,2048]{1,0:T(8,128)(2,1)} %get-tuple-element.15.refs_0_, f32[1,128]{1,0:T(1,128)} %get-tuple-element.16.refs_1_, ...), custom_call_target="tpu_custom_call" | custom-call | tf_op jit(solution)/shard_map/pallas_call | solution.py:773

commit v5 on v4

--- a/solution.py
+++ b/solution.py
@@ -89,6 +89,7 @@
     columns_in,
     line_rows,
     line_gate,
+    line_sum,
     grads,
     parts,
     far1,
@@ -369,19 +370,24 @@
         for h, k in ready[s]:
             rings[0, h][0][k].start()
 
-    def line_grad(t, h):
-        n = 2 * t + h
-        mine = (d_gate, d_up)[t - 1]
+    def line_rows_of(h, r):
+        return jnp.concatenate([line_rows[h, r, k] for k in range(SIDE)], axis=1)
+
+    def line_near(t, h):
+        grad = (d_gate, d_up)[t - 1]
         here = [columns_in[gx, k] if h == 0 else columns_in[k, gy] for k in range(SIDE)]
         total = mm(
-            mine[h * rows_h : (h + 1) * rows_h, :], jnp.concatenate(here, axis=1), NN
-        )
-        for r in range(SIDE - 1):
-            rows = jnp.concatenate([line_rows[h, r, k] for k in range(SIDE)], axis=1)
-            total = total + mm(line_gate[t - 1, h, r], rows, NN)
+            grad[h * rows_h : (h + 1) * rows_h, :], jnp.concatenate(here, axis=1), NN
+        )
+        for r in (0, 2):
+            total = total + mm(line_gate[t - 1, h, r], line_rows_of(h, r), NN)
+        line_sum[t - 1, h] = total
+
+    def line_far(t, h):
+        total = line_sum[t - 1, h] + mm(line_gate[t - 1, h, 1], line_rows_of(h, 1), NN)
         total = total.astype(BF16)
         for k in range(SIDE):
-            parts[n, k] = total[:, k * 128 : (k + 1) * 128]
+            parts[2 * t + h, k] = total[:, k * 128 : (k + 1) * 128]
 
     def ring(t, h):
         n = 2 * t + h
@@ -516,20 +522,26 @@
     inner = backward(0)
     for i in range(1, 4):
         inner = inner + backward(i)
-    gate_copies = []
+    gate_copies, forwards = {}, {}
     for t, grad in ((1, d_gate), (2, d_up)):
-        for by in (2, 1, 3):
-            for h in range(2):
-                gate_copies.append(
-                    line_copy(
-                        grad.at[pl.ds(h * rows_h, rows_h)],
-                        line_gate.at[t - 1, h, by - 1],
-                        6 * t + 3 * h + by - 1,
-                        h,
-                        by,
-                    )
+        for h in range(2):
+            for side, by in ((0, 1), (1, 3)):
+                gate_copies[t, h, side] = line_copy(
+                    grad.at[pl.ds(h * rows_h, rows_h)],
+                    line_gate.at[t - 1, h, by - 1],
+                    8 * t + 4 * h + side,
+                    h,
+                    by,
                 )
-    for c in gate_copies:
+                piece = pl.ds(side * rows_q, rows_q)
+                forwards[t, h, side] = line_copy(
+                    line_gate.at[t - 1, h, by - 1, piece],
+                    line_gate.at[t - 1, h, 1, piece],
+                    8 * t + 4 * h + 2 + side,
+                    h,
+                    by,
+                )
+    for c in gate_copies.values():
         c.start()
     left, right = inner[:, : cap // 2], inner[:, cap // 2 :]
     mine = jnp.where(core == 0, left, right)
@@ -608,16 +620,22 @@
             send_home(i - 1)
     down_grad(SIDE - 1)
     send_home(CHUNKS - 1)
+    for key, c in gate_copies.items():
+        c.wait_recv()
+        forwards[key].start()
+    run(0, 1)
+    for c in row_copies:
+        c.wait_recv()
+    for t in (1, 2):
+        for h in range(2):
+            line_near(t, h)
     inner_copy.wait_recv()
     dcomb_ref[...] = mine + inner_r[0:1, :]
-    for c in row_copies:
-        c.wait_recv()
-    run(0, 1)
     for t in (1, 2):
-        for c in gate_copies[6 * (t - 1) : 6 * t]:
-            c.wait_recv()
         for h in range(2):
-            line_grad(t, h)
+            for side in range(2):
+                forwards[t, h, side].wait_recv()
+            line_far(t, h)
             rings[t, h][6]()
     run(0, 2)
     run(1, 3)
@@ -655,7 +673,7 @@
         to_sibling(recv_a, fa_send, a_recv, j).wait_send()
         for s in range(SIDE):
             to_sibling(recv_b, fb_send, b_recv, j, s).wait_send()
-    for c in row_copies + gate_copies:
+    for c in [*row_copies, *gate_copies.values(), *forwards.values()]:
         c.wait_send()
     inner_copy.wait_send()
     for c in sib_copies:
@@ -732,6 +750,7 @@
                 pltpu.VMEM((SIDE, SIDE, cap, 128), BF16),
                 pltpu.VMEM((2, SIDE - 1, SIDE, cap, 128), BF16),
                 pltpu.VMEM((2, 2, SIDE - 1, rows_h, cap), BF16),
+                pltpu.VMEM((2, 2, rows_h, width // SIDE), F32),
                 pltpu.VMEM((2, SIDE * SIDE, rows_h, 128), BF16),
                 pltpu.VMEM((6, SIDE, rows_h, 128), BF16),
                 pltpu.VMEM((2, 2, 2, rows_h, 128), BF16),
@@ -751,8 +770,8 @@
                 dma((1 + CHUNKS,)),
                 dma((72,)),
                 dma((72,)),
-                dma((18,)),
-                dma((18,)),
+                dma((24,)),
+                dma((24,)),
             ],
             compiler_params=pltpu.CompilerParams(
                 collective_id=0, has_side_effects=True, vmem_limit_bytes=60 * 1024 * 1024

time: 105 us -> 101 us (0.962)
  Pallas kernels: 104 us -> 100 us
    pallas_call x1, Pallas kernels: 102 us -> 98.1 us  [on_device(): pl.pallas_call(functools.partial(layer_kernel, nz), out_shape=(jax.ShapeD...]
where the time goes in v5:
time: 101 us
  Pallas kernels  100 us (99%)
    pallas_call x1, Pallas kernels, on_device(): pl.pallas_call(functools.partial(layer_kernel, nz), out_shape=(jax.ShapeD...  98.1 us
    pallas_call x1, Pallas kernels, on_device(): pl.pallas_call(copy_kernel, out_shape=tuple((jax.ShapeDtypeStruct(o.shape...  2.21 us

profile of v5, /device:TPU:1, one launch (start us, length us, event | category | flops | bytes accessed | tf_op | source)
XLA Modules:
  0.0 101.0 jit_solution(17374038264308836974)
XLA Ops:
  0.6 98.1 %shard_map.146 = (bf16[128,2048]{1,0:T(8,128)(2,1)}, f32[1,128]{1,0:T(1,128)}, bf16[704,128]{1,0:T(8,128)(2,1)}, bf16[704,128]{1,0:T(8,128)(2,1)}, bf16[704,128]{1,0:T(8,128)(2,1)}) custom-call(bf16[128,2048]{1,0:T(8,128)(2,1)} %tok_ref.1, bf16[128,2048]{1,0:T(8,128)(2,1)} %cot_ref.1, s32[1,128]{1,0:T(1,128)} %bitcast.15, f32[16,2048]{1,0:T(8,128)} %shift_ref.1, ...), custom_call_target="tpu_custom_call" | custom-call | tf_op jit(solution)/shard_map/pallas_call | solution.py:705
  98.7 2.2 %shard_map.147 = (bf16[128,2048]{1,0:T(8,128)(2,1)}, f32[1,128]{1,0:T(1,128)}, bf16[704,128]{1,0:T(8,128)(2,1)}, bf16[704,128]{1,0:T(8,128)(2,1)}, bf16[704,128]{1,0:T(8,128)(2,1)}) custom-call(bf16[128,2048]{1,0:T(8,128)(2,1)} %get-tuple-element.15.refs_0_, f32[1,128]{1,0:T(1,128)} %get-tuple-element.16.refs_1_, ...), custom_call_target="tpu_custom_call" | custom-call | tf_op jit(solution)/shard_map/pallas_call | solution.py:792

commit v6 on v5

--- a/solution.py
+++ b/solution.py
@@ -138,7 +138,7 @@
             return {"grp": lax.rem(gx + by, SIDE) * SIDE + gy, "exp": me}
         return {"grp": gx * SIDE + lax.rem(gy + by, SIDE), "exp": me}
 
-    hops = [1, 7, 2, 6, 3, 5, 4] if nz == 8 else list(range(1, nz))
+    hops = [4, 3, 5, 2, 6, 1, 7] if nz == 8 else list(range(1, nz))
 
     loads = [
         pltpu.make_async_copy(src, dst, w_sem.at[i])
@@ -511,6 +511,8 @@
         loop(4, functools.partial(raw_sum, s))
         if s < SIDE - 1:
             down_grad(s)
+        if s == 2:
+            rings[0, 0][1]()
 
     def backward(i):
         at = pl.ds(i * rows_q, rows_q)
@@ -623,7 +625,7 @@
     for key, c in gate_copies.items():
         c.wait_recv()
         forwards[key].start()
-    run(0, 1)
+    rings[0, 1][1]()
     for c in row_copies:
         c.wait_recv()
     for t in (1, 2):

time: 101 us -> 100 us (0.990)
    pallas_call x1, Pallas kernels: 98.1 us -> 97.1 us  [on_device(): pl.pallas_call(functools.partial(layer_kernel, nz), out_shape=(jax.ShapeD...]
where the time goes in v6:
time: 100 us; the launch traced here: 99.9 us
  Pallas kernels  99.3 us (99%)
    pallas_call x1, Pallas kernels, on_device(): pl.pallas_call(functools.partial(layer_kernel, nz), out_shape=(jax.ShapeD...  97.1 us
    pallas_call x1, Pallas kernels, on_device(): pl.pallas_call(copy_kernel, out_shape=tuple((jax.ShapeDtypeStruct(o.shape...  2.21 us

profile of v6, /device:TPU:1, one launch (start us, length us, event | category | flops | bytes accessed | tf_op | source)
XLA Modules:
  0.0 99.9 jit_solution(17427475265420496509)
XLA Ops:
  0.6 97.1 %shard_map.146 = (bf16[128,2048]{1,0:T(8,128)(2,1)}, f32[1,128]{1,0:T(1,128)}, bf16[704,128]{1,0:T(8,128)(2,1)}, bf16[704,128]{1,0:T(8,128)(2,1)}, bf16[704,128]{1,0:T(8,128)(2,1)}) custom-call(bf16[128,2048]{1,0:T(8,128)(2,1)} %tok_ref.1, bf16[128,2048]{1,0:T(8,128)(2,1)} %cot_ref.1, s32[1,128]{1,0:T(1,128)} %bitcast.15, f32[16,2048]{1,0:T(8,128)} %shift_ref.1, ...), custom_call_target="tpu_custom_call" | custom-call | tf_op jit(solution)/shard_map/pallas_call | solution.py:707
  97.7 2.2 %shard_map.147 = (bf16[128,2048]{1,0:T(8,128)(2,1)}, f32[1,128]{1,0:T(1,128)}, bf16[704,128]{1,0:T(8,128)(2,1)}, bf16[704,128]{1,0:T(8,128)(2,1)}, bf16[704,128]{1,0:T(8,128)(2,1)}) custom-call(bf16[128,2048]{1,0:T(8,128)(2,1)} %get-tuple-element.15.refs_0_, f32[1,128]{1,0:T(1,128)} %get-tuple-element.16.refs_1_, ...), custom_call_target="tpu_custom_call" | custom-call | tf_op jit(solution)/shard_map/pallas_call | solution.py:794

commit v7 on v6

--- a/solution.py
+++ b/solution.py
@@ -300,13 +300,14 @@
     place_t[...] = place_f.T.astype(BF16)
 
     for j in hops:
-        from_peer(recv_a, a_send, a_recv, j).wait_recv()
-        to_sibling(recv_a, fa_send, a_recv, j).start()
         to_peer(send_a, recv_a, a_send, a_recv, j).wait_send()
         to_peer(send_b, recv_b, b_send, b_recv, j, 0).start()
     for s in range(1, SIDE):
         for j in hops:
             to_peer(send_b, recv_b, b_send, b_recv, j, s).start()
+    for j in hops:
+        from_peer(recv_a, a_send, a_recv, j).wait_recv()
+        to_sibling(recv_a, fa_send, a_recv, j).start()
     for j in [0] + hops:
         from_sibling(recv_a, fa_send, a_recv, j).wait_recv()
 

time: 100 us -> 100 us (level)
  no operation moved by 1% of the time
where the time goes in v7:
time: 100 us
  Pallas kernels  99.4 us (99%)
    pallas_call x1, Pallas kernels, on_device(): pl.pallas_call(functools.partial(layer_kernel, nz), out_shape=(jax.ShapeD...  97.2 us
    pallas_call x1, Pallas kernels, on_device(): pl.pallas_call(copy_kernel, out_shape=tuple((jax.ShapeDtypeStruct(o.shape...  2.21 us

profile of v7, /device:TPU:1, one launch (start us, length us, event | category | flops | bytes accessed | tf_op | source)
XLA Modules:
  0.0 100.1 jit_solution(2349771071360621090)
XLA Ops:
  0.6 97.2 %shard_map.146 = (bf16[128,2048]{1,0:T(8,128)(2,1)}, f32[1,128]{1,0:T(1,128)}, bf16[704,128]{1,0:T(8,128)(2,1)}, bf16[704,128]{1,0:T(8,128)(2,1)}, bf16[704,128]{1,0:T(8,128)(2,1)}) custom-call(bf16[128,2048]{1,0:T(8,128)(2,1)} %tok_ref.1, bf16[128,2048]{1,0:T(8,128)(2,1)} %cot_ref.1, s32[1,128]{1,0:T(1,128)} %bitcast.15, f32[16,2048]{1,0:T(8,128)} %shift_ref.1, ...), custom_call_target="tpu_custom_call" | custom-call | tf_op jit(solution)/shard_map/pallas_call | solution.py:708
  97.9 2.2 %shard_map.147 = (bf16[128,2048]{1,0:T(8,128)(2,1)}, f32[1,128]{1,0:T(1,128)}, bf16[704,128]{1,0:T(8,128)(2,1)}, bf16[704,128]{1,0:T(8,128)(2,1)}, bf16[704,128]{1,0:T(8,128)(2,1)}) custom-call(bf16[128,2048]{1,0:T(8,128)(2,1)} %get-tuple-element.15.refs_0_, f32[1,128]{1,0:T(1,128)} %get-tuple-element.16.refs_1_, ...), custom_call_target="tpu_custom_call" | custom-call | tf_op jit(solution)/shard_map/pallas_call | solution.py:795
